TPU v7x, 128 devices: a whole 4x4x4 slice. The times are simulated.
128 devices in a mesh: grp: 4 (over x), leaf: 32 (over z, y, core).
Axes of the slice: x: 4, y: 4, z: 4, core: 2. Of those that a mesh axis runs over, the one named last changes fastest.
Arguments:
- potentials: float32 [131072, 256], P(('grp', 'leaf')), may hold values from -16 to 16, as said below
- leaf_panels: int32 [128, 1024], P(('grp', 'leaf')), may hold values from 0 to 1023, each once within a row
- near_blocks: bfloat16 [49152, 128, 128], P(('grp', 'leaf')), may hold values from -0.125 to 0.125
- near_target: int32 [128, 384], P(('grp', 'leaf')), may hold values from 0 to 7
- near_source: int32 [128, 384], P(('grp', 'leaf')), may hold values from 0 to 23, as said below
- near_count: int32 [128], P(('grp', 'leaf')), may hold values from 48 to 384, as said below
- leaf_basis: bfloat16 [1024, 64, 128], P(('grp', 'leaf')), may hold values from -0.5 to 0.5
- far_leaf: bfloat16 [24576, 64, 64], P(('grp', 'leaf')), may hold values from -0.15625 to 0.15625
- far_leaf_target: int32 [128, 192], P(('grp', 'leaf')), may hold values from 0 to 7
- far_leaf_source: int32 [128, 192], P(('grp', 'leaf')), may hold values from 0 to 23, as said below
- leaf_transfer: bfloat16 [1024, 64, 64], P(('grp', 'leaf')), may hold values from -0.375 to 0.375
- leaf_parent: int32 [1024], P(('grp', 'leaf')), may hold values from 0 to 31
- far_two: bfloat16 [2048, 64, 64], P(('grp', 'leaf')), may hold values from -0.125 to 0.125
- far_two_target: int32 [128, 16], P(('grp', 'leaf')), may hold values from 0 to 31
- far_two_source: int32 [128, 16], P(('grp', 'leaf')), may hold values from 0 to 127
- two_transfer: bfloat16 [128, 64, 64], replicated, may hold values from -0.375 to 0.375
- two_parent: int32 [128], replicated, may hold values from 0 to 15
- far_one: bfloat16 [32, 64, 64], replicated, may hold values from -0.5 to 0.5
- far_one_target: int32 [32], replicated, may hold values from 0 to 15
- far_one_source: int32 [32], replicated, may hold values from 0 to 15
Outputs:
- solution: float32 [131072, 256], P(('grp', 'leaf'))
- residual_estimate: float32 [256], replicated
Inputs may be any that keep to these rules, and one draw needn't show every extreme that they name: `potentials`: entries of order one, larger towards later panels. `near_source`: window index: values below 8 name the previous device's leaves, from 16 the next device's; the first device names none before it, the last none after it. `far_leaf_source`: window index as for near_source, with the same rule at the two end devices. Slots of a device from near_count on hold no block; some device is full.
All inputs are finite; a program needn't handle non-finite values.
Results may differ from a plain program's by a relative error of at most 0.009.
Values may be sent and summed in bfloat16 or wider, within the bound.
A program may use at most 192 MiB of HBM per device.

v0:
```python
import jax
import jax.numpy as jnp
from jax import lax
from jax.sharding import PartitionSpec as P

P_SIZE = 128
CHILDREN = 8


EPS = 1e-06
HIGH = lax.Precision.HIGHEST


def padded(cells, sides, width):
    for axis, dim in sides:
        count = lax.axis_size(axis)
        ends = count - 1
        head = lax.slice_in_dim(cells, 0, width, axis=dim)
        tail = lax.slice_in_dim(cells, cells.shape[dim] - width, cells.shape[dim], axis=dim)
        cells = jnp.concatenate(
            [
                lax.ppermute(tail, axis, [(i, (i + 1) % count) for i in range(ends)]),
                cells,
                lax.ppermute(head, axis, [((i + 1) % count, i) for i in range(ends)]),
            ],
            axis=dim,
        )
    return cells


def indicator(values, count):
    return (values[None, :] == jnp.arange(count, dtype=jnp.int32)[:, None]).astype(jnp.float32)


def column_sum(values):
    return jnp.sum(values, axis=0)


def least_squares(beta_norm, first_diag, first_below, second_top, second_diag, second_below):
    first_radius = jnp.sqrt(first_diag * first_diag + first_below * first_below)
    first_cos = first_diag / first_radius
    first_sin = first_below / first_radius
    upper_term = first_cos * second_top + first_sin * second_diag
    lower_term = first_cos * second_diag - first_sin * second_top
    second_radius = jnp.sqrt(lower_term * lower_term + second_below * second_below)
    second_cos = lower_term / second_radius
    second_sin = second_below / second_radius
    weight_two = -first_sin * beta_norm * second_cos / second_radius
    weight_one = (first_cos * beta_norm - upper_term * weight_two) / first_radius
    return (weight_one, weight_two, first_sin * second_sin * beta_norm)


def on_device(
    potentials,
    leaf_panels,
    near_blocks,
    near_target,
    near_source,
    near_count,
    leaf_basis,
    far_leaf,
    far_leaf_target,
    far_leaf_source,
    leaf_transfer,
    leaf_parent,
    far_two,
    far_two_target,
    far_two_source,
    two_transfer,
    two_parent,
    far_one,
    far_one_target,
    far_one_source,
):
    leaves = leaf_basis.shape[0]
    columns = potentials.shape[1]
    window_len = 3 * leaves
    panel_order = leaf_panels[0]
    per_group = two_transfer.shape[0] // lax.axis_size("grp")
    top_count = two_transfer.shape[0] // CHILDREN
    group_index = lax.axis_index("grp")
    group_rows = lax.dynamic_slice_in_dim(two_transfer, group_index * per_group, per_group, 0)
    group_parent = lax.dynamic_slice_in_dim(two_parent, group_index * per_group, per_group, 0)
    slot_total = near_target.shape[1]
    alive_mask = jnp.arange(slot_total, dtype=jnp.int32) < near_count[0]
    pair_keys = jnp.where(alive_mask, near_target[0] * window_len + near_source[0], -1)
    pair_select = indicator(pair_keys, leaves * window_len).astype(jnp.bfloat16)
    combined = jnp.dot(
        pair_select,
        near_blocks.reshape(slot_total, P_SIZE * P_SIZE),
        preferred_element_type=jnp.float32,
    )
    combined = combined.reshape(leaves, window_len, P_SIZE, P_SIZE)
    leaf_select = indicator(far_leaf_target[0], leaves)
    parent_select = indicator(leaf_parent, per_group)
    one_select = indicator(far_one_target, top_count)
    upward_select = indicator(two_parent, top_count)
    two_select = indicator(far_two_target[0], per_group)
    two_source = far_two_source[0]

    def upper_levels(sources):
        rising = jnp.einsum(
            "cab,car->cbr", two_transfer, sources, preferred_element_type=jnp.float32
        )
        level_one = jnp.einsum("uc,cbr->ubr", upward_select, rising, precision=HIGH).astype(
            jnp.bfloat16
        )
        pieces = jnp.einsum(
            "jab,jbr->jar",
            far_one,
            jnp.take(level_one, far_one_source, axis=0),
            preferred_element_type=jnp.float32,
        )
        local_one = jnp.einsum("uj,jar->uar", one_select, pieces, precision=HIGH).astype(
            jnp.bfloat16
        )
        falling = jnp.einsum(
            "cab,cbr->car",
            group_rows,
            jnp.take(local_one, group_parent, axis=0),
            preferred_element_type=jnp.float32,
        )
        pieces_two = jnp.einsum(
            "jab,jbr->jar",
            far_two,
            jnp.take(sources, two_source, axis=0),
            preferred_element_type=jnp.float32,
        )
        return (jnp.einsum("cj,jar->car", two_select, pieces_two, precision=HIGH), falling)

    def apply(vector_in):
        leaf_lined = jnp.take(vector_in.astype(jnp.bfloat16), panel_order, axis=0).reshape(
            leaves, P_SIZE, columns
        )
        coeffs = jnp.einsum(
            "lkp,lpr->lkr", leaf_basis, leaf_lined, preferred_element_type=jnp.float32
        ).astype(jnp.bfloat16)
        window = padded(
            jnp.concatenate([leaf_lined, coeffs], axis=1), ((("grp", "leaf"), 0),), leaves
        )
        panels_window = window[:, :P_SIZE].astype(jnp.float32)
        coeff_window = window[:, P_SIZE:]
        near_part = jnp.einsum("tspq,sqr->tpr", combined, panels_window, precision=HIGH)
        pieces = jnp.einsum(
            "jab,jbr->jar",
            far_leaf,
            jnp.take(coeff_window, far_leaf_source[0], axis=0),
            preferred_element_type=jnp.float32,
        )
        leaf_local = jnp.einsum("tj,jar->tar", leaf_select, pieces, precision=HIGH)
        rising = jnp.einsum(
            "lab,lar->lbr", leaf_transfer, coeffs, preferred_element_type=jnp.float32
        )
        partial_value = jnp.einsum("cl,lbr->cbr", parent_select, rising, precision=HIGH)
        group_total = lax.psum(partial_value, "leaf").astype(jnp.bfloat16)
        sources = lax.all_gather(group_total, "grp", axis=0, tiled=True)
        far_sum, falling = upper_levels(sources)
        level_two = (lax.psum(far_sum, "leaf") + falling).astype(jnp.bfloat16)
        merged = leaf_local + jnp.einsum(
            "lab,lbr->lar",
            leaf_transfer,
            jnp.take(level_two, leaf_parent, axis=0),
            preferred_element_type=jnp.float32,
        )
        merged = merged.astype(jnp.bfloat16)
        result = near_part + jnp.einsum(
            "lkp,lkr->lpr", leaf_basis, merged, preferred_element_type=jnp.float32
        )
        return (
            jnp.zeros((leaves * P_SIZE, columns), jnp.float32)
            .at[panel_order]
            .set(result.reshape(-1, columns))
        )

    start = lax.psum(column_sum(potentials * potentials), ("grp", "leaf"))
    beta_norm = jnp.sqrt(start + EPS)
    first = potentials / beta_norm
    image = apply(first)
    first_diag = lax.psum(column_sum(first * image), ("grp", "leaf"))
    rest = image - first_diag * first
    first_below = jnp.sqrt(lax.psum(column_sum(rest * rest), ("grp", "leaf")) + EPS)
    second = rest / first_below
    image_two = apply(second)
    second_top = lax.psum(column_sum(first * image_two), ("grp", "leaf"))
    rest_two = image_two - second_top * first
    second_diag = lax.psum(column_sum(second * rest_two), ("grp", "leaf"))
    rest_two = rest_two - second_diag * second
    second_below = jnp.sqrt(lax.psum(column_sum(rest_two * rest_two), ("grp", "leaf")) + EPS)
    weight_one, weight_two, estimate = least_squares(
        beta_norm, first_diag, first_below, second_top, second_diag, second_below
    )
    return (weight_one * first + weight_two * second, estimate)


def solution(mesh):
    in_specs = (
        P(("grp", "leaf"), None),
        P(("grp", "leaf"), None),
        P(("grp", "leaf"), None, None),
        P(("grp", "leaf"), None),
        P(("grp", "leaf"), None),
        P(("grp", "leaf")),
        P(("grp", "leaf"), None, None),
        P(("grp", "leaf"), None, None),
        P(("grp", "leaf"), None),
        P(("grp", "leaf"), None),
        P(("grp", "leaf"), None, None),
        P(("grp", "leaf")),
        P(("grp", "leaf"), None, None),
        P(("grp", "leaf"), None),
        P(("grp", "leaf"), None),
        P(),
        P(),
        P(),
        P(),
        P(),
    )
    out_specs = (P(("grp", "leaf"), None), P())
    return jax.shard_map(
        on_device, mesh=mesh, in_specs=in_specs, out_specs=out_specs, check_vma=False
    )
```

profile of v0, /device:TPU:0, one launch (start us, length us, event | category | flops | bytes accessed | tf_op | source)
XLA Modules:
  0.0 1198.6 jit_solution(11979110309957959971)
XLA Ops:
  10.0 68.2 %psum.70 = f32[256]{0:T(256)S(1)} all-reduce(f32[256]{0:T(256)S(1)} %multiply_reduce_fusion.5), channel_id=1, replica_groups=mesh['grp'=4,'leaf'=32] {'grp','leaf'}, use_global_device_ids=true, to_apply=%region_1.2 | all-reduce | flops 256 | bytes 2048 | tf_op jit(solution)/shard_map/psum | solution.py:175
  92.1 152.6 %all-reduce.8 = bf16[32,64,256]{2,0,1:T(8,128)(2,1)} all-reduce(f32[32,64,256]{2,0,1:T(8,128)S(1)} %fusion.84), channel_id=1, replica_groups=mesh['grp'=4,'leaf'=32] {'leaf'}, use_global_device_ids=true, to_apply=%region_2.0 | all-reduce | flops 524288 | bytes 3145728 | tf_op jit(solution)/shard_map/psum | solution.py:155
  245.8 15.1 %copy.174 = bf16[48,8,128,128]{3,1,2,0:T(8,128)(2,1)} copy(bf16[48,8,128,128]{3,2,1,0:T(8,128)(2,1)} %bitcast.140) | data formatting | bytes 25165824
  261.0 15.9 %copy.66 = bf16[16384,384]{1,0:T(8,128)(2,1)} copy(bf16[16384,384]{0,1:T(8,128)(2,1)} %bitcast.131) | data formatting | bytes 25165824 | tf_op jit(solution)/shard_map/dot_general | solution.py:88
  280.7 11.1 fusion.109
  309.4 8.6 gather_fusion.1
  321.3 9.2 fusion.18
  349.7 7.5 fusion.50
  364.9 82.0 %all-reduce.5.cloned.1.call-done = f32[32,64,256]{2,0,1:T(8,128)} async-done(((f32[32,64,256]{2,0,1:T(8,128)}), f32[32,64,256]{2,0,1:T(8,128)}) %all-reduce.5.cloned.1.call-update) | async-done | bytes 2097168 | tf_op jit(solution)/shard_map/psum | solution.py:158
  451.1 15.5 %fusion.65 = bf16[8,64,256]{2,0,1:T(8,128)(2,1)S(1)} fusion(f32[192,64,256]{2,1,0:T(8,128)} %fusion.18, f32[8,256,64]{1,2,0:T(8,128)S(1)} %fusion.102, s32[192]{0:T(256)S(1)} %bitcast.154), kind=kOutput, calls=%fused_computation.72 | convolution fusion | flops 302253568 | bytes 13370112 | tf_op jit(solution)/shard_map/tj,jar->tar/dot_general | solution.py:150
  467.1 12.4 %fusion.41 = f32[8,128,256]{2,1,0:T(8,128)} fusion(f32[8,128,256]{2,1,0:T(8,128)S(1)} %convolution_bitcast_fusion.5, bf16[24,192,256]{2,1,0:T(8,128)(2,1)S(1)} %copy-done.8, f32[8,24,128,128]{3,1,2,0:T(8,128)} %fusion.109), kind=kOutput, calls=%fused_computation.60 | convolution fusion | flops 9663938560 | bytes 16252928 | tf_op jit(solution)/shard_map/tspq,sqr->tpr/dot_general | solution.py:143
  485.4 65.7 %psum.73 = f32[256]{0:T(256)S(1)} all-reduce(f32[256]{0:T(256)S(1)} %multiply_reduce_fusion.4), channel_id=1, replica_groups=mesh['grp'=4,'leaf'=32] {'grp','leaf'}, use_global_device_ids=true, to_apply=%region_6.12 | all-reduce | flops 256 | bytes 2048 | tf_op jit(solution)/shard_map/psum | solution.py:179
  551.4 62.4 %psum.74 = f32[256]{0:T(256)S(1)} all-reduce(f32[256]{0:T(256)S(1)} %multiply_reduce_fusion.3), channel_id=1, replica_groups=mesh['grp'=4,'leaf'=32] {'grp','leaf'}, use_global_device_ids=true, to_apply=%region_8.14 | all-reduce | flops 256 | bytes 2048 | tf_op jit(solution)/shard_map/psum | solution.py:181
  625.5 148.8 %all-reduce.9 = bf16[32,64,256]{2,0,1:T(8,128)(2,1)} all-reduce(f32[32,64,256]{2,0,1:T(8,128)} %fusion.82), channel_id=1, replica_groups=mesh['grp'=4,'leaf'=32] {'leaf'}, use_global_device_ids=true, to_apply=%region_9.15 | all-reduce | flops 524288 | bytes 3145728 | tf_op jit(solution)/shard_map/psum | solution.py:155
  782.6 8.4 gather_fusion.7
  794.4 9.2 fusion.21
  803.6 18.1 %all-gather.5.cloned.1.call-done = bf16[128,64,256]{2,0,1:T(8,128)(2,1)} async-done(((bf16[32,64,256]{2,0,1:T(8,128)(2,1)}), bf16[128,64,256]{2,0,1:T(8,128)(2,1)}) %all-gather.5.cloned.1.call-update) | async-done | bytes 4194320 | tf_op jit(solution)/shard_map/all_gather | solution.py:156
  841.4 7.9 fusion.53
  860.2 89.8 %all-reduce.7.cloned.1.call-done = f32[32,64,256]{2,0,1:T(8,128)} async-done(((f32[32,64,256]{2,0,1:T(8,128)}), f32[32,64,256]{2,0,1:T(8,128)}) %all-reduce.7.cloned.1.call-update) | async-done | bytes 2097168 | tf_op jit(solution)/shard_map/psum | solution.py:158
  957.9 15.7 %fusion.62 = bf16[8,64,256]{2,0,1:T(8,128)(2,1)S(1)} fusion(f32[192,64,256]{2,1,0:T(8,128)} %fusion.21, f32[8,256,64]{1,2,0:T(8,128)S(1)} %fusion.100, s32[192]{0:T(256)S(1)} %bitcast.155), kind=kOutput, calls=%fused_computation.71 | convolution fusion | flops 302253568 | bytes 13370112 | tf_op jit(solution)/shard_map/tj,jar->tar/dot_general | solution.py:150
  973.9 12.3 %fusion.38 = f32[8,128,256]{2,1,0:T(8,128)} fusion(f32[8,128,256]{2,1,0:T(8,128)S(1)} %convolution_bitcast_fusion.4, bf16[24,192,256]{2,1,0:T(8,128)(2,1)S(1)} %copy-done.7, f32[8,24,128,128]{3,1,2,0:T(8,128)} %fusion.109), kind=kOutput, calls=%fused_computation.59 | convolution fusion | flops 9663938560 | bytes 16252928 | tf_op jit(solution)/shard_map/tspq,sqr->tpr/dot_general | solution.py:143
  994.2 65.7 %psum.77 = f32[256]{0:T(256)S(1)} all-reduce(f32[256]{0:T(256)S(1)} %multiply_reduce_fusion.2), channel_id=1, replica_groups=mesh['grp'=4,'leaf'=32] {'grp','leaf'}, use_global_device_ids=true, to_apply=%region_13.19 | all-reduce | flops 256 | bytes 2048 | tf_op jit(solution)/shard_map/psum | solution.py:184
  1061.4 62.4 %psum.78 = f32[256]{0:T(256)S(1)} all-reduce(f32[256]{0:T(256)S(1)} %multiply_reduce_fusion.1), channel_id=1, replica_groups=mesh['grp'=4,'leaf'=32] {'grp','leaf'}, use_global_device_ids=true, to_apply=%region_15.21 | all-reduce | flops 256 | bytes 2048 | tf_op jit(solution)/shard_map/psum | solution.py:186
  1125.4 64.5 %psum.79 = f32[256]{0:T(256)S(1)} all-reduce(f32[256]{0:T(256)S(1)} %multiply_reduce_fusion), channel_id=1, replica_groups=mesh['grp'=4,'leaf'=32] {'grp','leaf'}, use_global_device_ids=true, to_apply=%region_17.23 | all-reduce | flops 256 | bytes 2048 | tf_op jit(solution)/shard_map/psum | solution.py:188
  (213 shorter events, 153.9 us)
Async XLA Ops:
  7.2 351.1 %copy-start = (bf16[32,64,64]{2,1,0:T(8,128)(2,1)S(1)}, bf16[32,64,64]{2,1,0:T(8,128)(2,1)}, u32[]{:S(2)}) copy-start(bf16[32,64,64]{2,1,0:T(8,128)(2,1)} %param.47) | copy-start | bytes 786436
  7.2 323.3 %all-gather.3.cloned.1.call-start = ((), (), s32[]{:S(2)}) async-start(), calls=%async_computation | async-start | bytes 5242880 | tf_op jit(solution)/shard_map/all_gather | solution.py:156
  8.0 75.6 %copy-start.26 = (pred[1024]{0:T(1024)(128)(4,1)}, pred[1024]{0:T(1024)(128)(4,1)S(1)}, u32[]{:S(2)}) copy-start(pred[1024]{0:T(1024)(128)(4,1)S(1)} %compare_and_fusion) | copy-start | bytes 3076
  85.5 222.7 %collective-permute-start.1 = (bf16[8,192,256]{2,1,0:T(8,128)(2,1)}, bf16[8,192,256]{2,1,0:T(8,128)(2,1)}, u32[]{:S(2)}, u32[]{:S(2)}) collective-permute-start(bf16[8,192,256]{2,1,0:T(8,128)(2,1)} %pad_maximum_fusion.4), channel_id=1, source_target_pairs={{1,0},{2,1},{3,2},{4,3},{5,4},{6,5},{7,6},{8,7},{9,8},{10,9},{11,1... | collective-permute-start | bytes 2359304 | tf_op jit(solution)/shard_map/ppermute | solution.py:24
  86.8 221.4 %collective-permute-start = (bf16[8,192,256]{2,1,0:T(8,128)(2,1)}, bf16[8,192,256]{2,1,0:T(8,128)(2,1)}, u32[]{:S(2)}, u32[]{:S(2)}) collective-permute-start(bf16[8,192,256]{2,1,0:T(8,128)(2,1)} %pad_maximum_fusion.4), channel_id=1, source_target_pairs={{0,1},{1,2},{2,3},{3,4},{4,5},{5,6},{6,7},{7,8},{8,9},{9,10},{10,1... | collective-permute-start | bytes 2359304 | tf_op jit(solution)/shard_map/ppermute | solution.py:22
  91.0 154.7 %copy-start.50 = (s32[1,192]{1,0:T(1,128)S(1)}, s32[1,192]{1,0:T(1,128)}, u32[]{:S(2)}) copy-start(s32[1,192]{1,0:T(1,128)} %param.39) | copy-start | bytes 2308
  244.7 202.1 %all-reduce.5.cloned.1.call-start = ((), (), s32[]{:S(2)}) async-start(), calls=%async_computation.1 | async-start | bytes 4194304 | tf_op jit(solution)/shard_map/psum | solution.py:158
  245.8 63.6 %copy-start.28 = (s32[1024]{0:T(1024)}, s32[1024]{0:T(1024)S(1)}, u32[]{:S(2)}) copy-start(s32[1024]{0:T(1024)S(1)} %pad_clamp_fusion.4) | copy-start | bytes 12292
  260.9 19.2 %copy-start.53 = (s32[32]{0:T(128)S(1)}, s32[32]{0:T(128)}, u32[]{:S(2)}) copy-start(s32[32]{0:T(128)} %param.49) | copy-start | bytes 388
  278.1 172.1 %copy-start.29 = (s32[1024]{0:T(1024)}, s32[1024]{0:T(1024)S(1)}, u32[]{:S(2)}) copy-start(s32[1024]{0:T(1024)S(1)} %pad_clamp_fusion) | copy-start | bytes 12292
  297.1 47.1 %copy-start.4 = (bf16[128,64,64]{1,2,0:T(8,128)(2,1)}, bf16[128,64,64]{1,2,0:T(8,128)(2,1)S(1)}, u32[]{:S(2)}) copy-start(bf16[128,64,64]{1,2,0:T(8,128)(2,1)S(1)} %copy.76) | copy-start | bytes 3145732
  344.0 477.8 %all-gather.5.cloned.1.call-start = ((), (), s32[]{:S(2)}) async-start(), calls=%async_computation.2 | async-start | bytes 5242880 | tf_op jit(solution)/shard_map/all_gather | solution.py:156
  364.9 85.9 %copy-start.39 = (pred[8]{0:T(512)(128)(4,1)S(1)}, pred[8]{0:T(512)(128)(4,1)}, u32[]{:S(2)}) copy-start(pred[8]{0:T(512)(128)(4,1)} %compare_and_fusion.1) | copy-start | bytes 28
  364.9 86.2 %copy-start.35 = (s32[1,192]{1,0:T(1,128)S(1)}, s32[1,192]{1,0:T(1,128)}, u32[]{:S(2)}) copy-start(s32[1,192]{1,0:T(1,128)} %param.38) | copy-start | bytes 2308
  620.8 153.5 %copy-start.6 = (bf16[1024,256]{1,0:T(8,128)(2,1)}, bf16[1024,256]{1,0:T(8,128)(2,1)S(1)}, u32[]{:S(2)}) copy-start(bf16[1024,256]{1,0:T(8,128)(2,1)S(1)} %broadcast_select_fusion) | copy-start | bytes 1572868
  622.1 152.3 %copy-start.10 = (bf16[8,256,64]{1,2,0:T(8,128)(2,1)}, bf16[8,256,64]{1,2,0:T(8,128)(2,1)S(1)}, u32[]{:S(2)}) copy-start(bf16[8,256,64]{1,2,0:T(8,128)(2,1)S(1)} %convolution_convert_fusion) | copy-start | bytes 786436
  774.3 175.7 %all-reduce.7.cloned.1.call-start = ((), (), s32[]{:S(2)}) async-start(), calls=%async_computation.3 | async-start | bytes 4194304 | tf_op jit(solution)/shard_map/psum | solution.py:158
  774.4 4.4 collective-permute-start.3
  775.7 4.9 collective-permute-start.2
  803.6 27.6 %copy-start.20 = (bf16[16,64,64]{2,1,0:T(8,128)(2,1)S(1)}, bf16[16,64,64]{2,1,0:T(8,128)(2,1)}, u32[]{:S(2)}) copy-start(bf16[16,64,64]{2,1,0:T(8,128)(2,1)} %param.42) | copy-start | bytes 393220
  803.6 28.6 %copy-start.43 = (s32[1,16]{1,0:T(1,128)S(1)}, s32[1,16]{1,0:T(1,128)}, u32[]{:S(2)}) copy-start(s32[1,16]{1,0:T(1,128)} %param.43) | copy-start | bytes 196
  860.2 97.6 %copy-start.36 = (s32[1,192]{1,0:T(1,128)S(1)}, s32[1,192]{1,0:T(1,128)}, u32[]{:S(2)}) copy-start(s32[1,192]{1,0:T(1,128)} %param.38) | copy-start | bytes 2308
  1059.9 130.1 %copy-start.23 = (f32[256]{0:T(256)S(1)}, f32[256]{0:T(256)}, u32[]{:S(2)}) copy-start(f32[256]{0:T(256)} %copy-done.22) | copy-start | bytes 3076
  1059.9 130.1 %copy-start.25 = (f32[256]{0:T(256)S(1)}, f32[256]{0:T(256)}, u32[]{:S(2)}) copy-start(f32[256]{0:T(256)} %copy-done.24) | copy-start | bytes 3076
  (38 other events, 307.7 us)
Sparse Core Ops, SparseCore 0:
  244.9 43.0 all-gather.2
  344.1 102.7 all-reduce.4
  774.4 47.2 all-gather.4
  835.3 114.6 all-reduce.6
where the time goes:
time: 1200 us
  blocking collectives  690 us (58%)
  waiting for transfers between devices  192 us (16%)
  matrix products  140 us (12%)
  local copies, waits for them, and re-layouts  116 us (10%)
  other arithmetic  34.1 us (3%)
  between operations  15.6 us (1%)
    psum x2, blocking collectives, apply(): group_total = lax.psum(partial_value, 'leaf').astype(jnp.bfloat16)  301 us
    psum x2, waiting for transfers between devices, apply(): level_two = (lax.psum(far_sum, 'leaf') + falling).astype(jnp.bfloat16)  172 us
    psum x1, blocking collectives, on_device(): start = lax.psum(column_sum(potentials * potentials), ('grp', 'leaf'))  68.2 us
    psum x1, blocking collectives, on_device(): first_diag = lax.psum(column_sum(first * image), ('grp', 'leaf'))  65.7 us
    psum x1, blocking collectives, on_device(): second_top = lax.psum(column_sum(first * image_two), ('grp', 'leaf'))  65.7 us
    psum x1, blocking collectives, on_device(): lax.psum(column_sum(rest_two * rest_two), ('grp', 'leaf')) + EPS  64.5 us
    psum x1, blocking collectives, on_device(): second_diag = lax.psum(column_sum(second * rest_two), ('grp', 'leaf'))  62.4 us
    psum x1, blocking collectives, on_device(): lax.psum(column_sum(rest * rest), ('grp', 'leaf')) + EPS  62.4 us
  transfers between devices with their start and end apart: 8, of which 4 were waited for; matrix products, arithmetic and copies ran while one was open for 13% of the time, Pallas kernels for 0%

commit v1 on v0

v1 whole, which is shorter than its diff:
```python
import jax
import jax.numpy as jnp
from jax import lax
from jax.experimental import pallas as pl
from jax.experimental.pallas import tpu as pltpu
from jax.sharding import PartitionSpec as P

P_SIZE = 128
K = 64
HALF = 128
EPS = 1e-06
BF = jnp.bfloat16
F32 = jnp.float32
MESH = pl.DeviceIdType.MESH
VMEM = pltpu.VMEM
DMA = pltpu.SemaphoreType.DMA
NEAR_STEPS = 8


def dot(a, b):
    return jnp.dot(a, b, preferred_element_type=F32)


def combine_kernel(
    near_target, near_source, near_count, far_target, far_source, near_ref, far_ref, c_ref, fl_ref, acc, facc
):
    step = pl.program_id(0)
    per_step = near_ref.shape[0]
    window = 24

    @pl.when(step == 0)
    def _():
        def zero(i, carry):
            acc[i] = jnp.zeros((P_SIZE, P_SIZE), F32)
            facc[i] = jnp.zeros((K, K), F32)
            return carry

        lax.fori_loop(0, acc.shape[0], zero, 0)

    live = jnp.clip(near_count[0] - step * per_step, 0, per_step)

    def add(j, carry):
        slot = step * per_step + j
        key = near_target[0, slot] * window + near_source[0, slot]
        acc[key] = acc[key] + near_ref[j].astype(F32)
        return carry

    lax.fori_loop(0, live, add, 0)

    @pl.when(step == pl.num_programs(0) - 1)
    def _():
        def add_far(j, carry):
            key = far_target[0, j] * window + far_source[0, j]
            facc[key] = facc[key] + far_ref[j].astype(F32)
            return carry

        lax.fori_loop(0, far_ref.shape[0], add_far, 0)

        def write(i, carry):
            t, s = i // window, i % window
            rows = pl.ds(pl.multiple_of(t * P_SIZE, P_SIZE), P_SIZE)
            lanes = pl.ds(pl.multiple_of(s * P_SIZE, P_SIZE), P_SIZE)
            c_ref[rows, lanes] = acc[i].astype(BF)
            return carry

        lax.fori_loop(0, acc.shape[0], write, 0)

        def write_far(i, carry):
            t, s = i // (window // 2), i % (window // 2)
            rows = pl.ds(pl.multiple_of(t * K, K), K)
            lanes = pl.ds(pl.multiple_of(s * 2 * K, 2 * K), 2 * K)
            both = jnp.concatenate([facc[2 * i], facc[2 * i + 1]], axis=1)
            fl_ref[rows, lanes] = both.astype(BF)
            return carry

        lax.fori_loop(0, facc.shape[0] // 2, write_far, 0)


def combine(near_target, near_source, near_count, far_target, far_source, near_blocks, far_leaf):
    smem = pl.BlockSpec(memory_space=pltpu.SMEM)
    slots = near_blocks.shape[0]
    per_step = slots // NEAR_STEPS
    return pl.pallas_call(
        combine_kernel,
        grid=(NEAR_STEPS,),
        out_shape=(
            jax.ShapeDtypeStruct((1024, 3072), BF),
            jax.ShapeDtypeStruct((512, 1536), BF),
        ),
        in_specs=[smem] * 5
        + [
            pl.BlockSpec((per_step, P_SIZE, P_SIZE), lambda i: (i, 0, 0)),
            pl.BlockSpec(far_leaf.shape, lambda i: (0, 0, 0)),
        ],
        out_specs=(
            pl.BlockSpec((1024, 3072), lambda i: (0, 0)),
            pl.BlockSpec((512, 1536), lambda i: (0, 0)),
        ),
        scratch_shapes=[VMEM((192, P_SIZE, P_SIZE), F32), VMEM((192, K, K), F32)],
        compiler_params=pltpu.CompilerParams(
            vmem_limit_bytes=56 * 1024 * 1024, dimension_semantics=("arbitrary",)
        ),
        cost_estimate=pl.CostEstimate(flops=10**7, bytes_accessed=20 * 10**6, transcendentals=0),
        name="combine",
    )(near_target, near_source, near_count, far_target, far_source, near_blocks, far_leaf)


def remote(src, dst, send, recv, device):
    return pltpu.make_async_remote_copy(
        src_ref=src, dst_ref=dst, send_sem=send, recv_sem=recv, device_id=device, device_id_type=MESH
    )


def place():
    x = lax.axis_index("grp")
    leaf = lax.axis_index("leaf")
    core = lax.rem(leaf, 2)
    chip = lax.div(leaf, 2)
    return x, lax.div(chip, 4), lax.rem(chip, 4), core


def leaf_of(z, y, core):
    return (z * 4 + y) * 2 + core


def apply_kernel(
    idx_s,
    v_ref,
    basis,
    falling_ref,
    c_hbm,
    fl_hbm,
    tv_hbm,
    s_hbm,
    down_hbm,
    w_ref,
    wb_ref,
    c_mat,
    fl_mat,
    tv_mat,
    s_mat,
    down_mat,
    win,
    cw,
    chalf,
    c2,
    local_half,
    rs_out,
    rs_in,
    q1x,
    q1,
    ag,
    gathered,
    far_out,
    far_in,
    l2,
    sib_out,
    sib_in,
    merged,
    load_sem,
    win_send,
    win_recv,
    sib_send,
    sib_recv,
    rs_send,
    rs_recv,
    q1x_send,
    q1x_recv,
    q1_send,
    q1_recv,
    ag_send,
    ag_recv,
    far_send,
    far_recv,
    l2_send,
    l2_recv,
):
    x, z, y, core = place()
    chip = z * 4 + y
    me = x * 32 + chip * 2 + core

    loads = [
        pltpu.make_async_copy(src, dst, load_sem.at[i])
        for i, (src, dst) in enumerate(
            ((tv_hbm, tv_mat), (c_hbm, c_mat), (fl_hbm, fl_mat), (s_hbm, s_mat), (down_hbm, down_mat))
        )
    ]
    for load in loads:
        load.start()

    sibling = (x, chip * 2 + 1 - core)
    before = (lax.div(me + 127, 32) % 4, lax.rem(me + 31, 32))
    after = (lax.div(me + 1, 32) % 4, lax.rem(me + 1, 32))
    has_before = me > 0
    has_after = me < 127

    def plane(k):
        tz = lax.rem(z + lax.div(k, 4), 4)
        ty = lax.rem(y + lax.rem(k, 4), 4)
        return tz * 4 + ty, (x, leaf_of(tz, ty, core))

    def along(axis, k):
        if axis == "x":
            return (lax.rem(x + k, 4), leaf_of(z, y, core))
        if axis == "y":
            return (x, leaf_of(z, lax.rem(y + k, 4), core))
        return (x, leaf_of(lax.rem(z + k, 4), y, core))

    barrier = pltpu.get_barrier_semaphore()

    def greet(k, carry):
        pl.semaphore_signal(barrier, inc=1, device_id=plane(k)[1], device_id_type=MESH)
        return carry

    lax.fori_loop(1, 16, greet, 0)
    for k in range(1, 4):
        pl.semaphore_signal(barrier, inc=1, device_id=along("x", k), device_id_type=MESH)
    pl.semaphore_signal(barrier, inc=1, device_id=sibling, device_id_type=MESH)

    @pl.when(has_before)
    def _():
        pl.semaphore_signal(barrier, inc=1, device_id=before, device_id_type=MESH)

    @pl.when(has_after)
    def _():
        pl.semaphore_signal(barrier, inc=1, device_id=after, device_id_type=MESH)

    win[pl.ds(1024, 1024), :] = v_ref[...]

    @pl.when(jnp.logical_not(has_before))
    def _():
        win[pl.ds(0, 1024), :] = jnp.zeros((1024, 256), BF)

    @pl.when(jnp.logical_not(has_after))
    def _():
        win[pl.ds(2048, 1024), :] = jnp.zeros((1024, 256), BF)

    def own_coeffs(i, carry):
        rows = pl.ds(pl.multiple_of(i * P_SIZE, P_SIZE), P_SIZE)
        part = dot(basis[8 + i], v_ref[rows, :]).astype(BF)
        into = pl.ds(pl.multiple_of(i * K, K), K)
        chalf[0, into, :] = part[:, :HALF]
        chalf[1, into, :] = part[:, HALF:]
        return carry

    lax.fori_loop(0, 8, own_coeffs, 0)
    c2[pl.ds(0, 512), :] = chalf[core]

    pl.semaphore_wait(barrier, 19 + has_before.astype(jnp.int32) + has_after.astype(jnp.int32))

    coeff_swap = remote(
        chalf.at[1 - core], c2.at[pl.ds(512, 512)], sib_send.at[0], sib_recv.at[0], sibling
    )
    coeff_swap.start()
    mine = win.at[pl.ds(1024, 1024)]
    to_after = remote(mine, win.at[pl.ds(0, 1024)], win_send.at[0], win_recv.at[0], after)
    to_before = remote(mine, win.at[pl.ds(2048, 1024)], win_send.at[1], win_recv.at[1], before)

    loads[0].wait()
    coeff_swap.wait_recv()

    def rs_copy(k):
        there, device = plane(k)
        return remote(rs_out.at[there], rs_in.at[k], rs_send.at[k], rs_recv.at[k], device)

    def rs_step(k, carry):
        there, _ = plane(k)
        rs_out[there] = dot(tv_mat[there], c2[...]).astype(BF)
        rs_copy(k).start()
        return carry

    lax.fori_loop(1, 16, rs_step, 0)
    rs_in[0] = dot(tv_mat[chip], c2[...]).astype(BF)

    @pl.when(has_after)
    def _():
        to_after.start()

    @pl.when(has_before)
    def _():
        to_before.start()

    def rs_sum(k, total):
        rs_copy(k).wait_recv()
        return total + rs_in[k].astype(F32)

    total = lax.fori_loop(1, 16, rs_sum, rs_in[0].astype(F32)).astype(BF)

    even = (z * 4 + y) * 4 + x
    odd = 64 + (y * 4 + x) * 4 + z
    ag[even] = total[0:K]
    ag[odd] = total[K : 2 * K]
    q1x[x] = total[2 * K : 3 * K]

    stages = (
        (0, 0, "x", even, 1),
        (1, 0, "z", odd, 1),
        (0, 1, "y", (z * 4 + y) * 4, 4),
        (1, 1, "x", 64 + (y * 4 + x) * 4, 4),
        (0, 2, "z", z * 16, 16),
        (1, 2, "y", 64 + y * 16, 16),
    )

    def ag_copy(number, k):
        _, _, axis, first, count = stages[number]
        part = ag.at[pl.ds(first, count)]
        i = number * 3 + k - 1
        return remote(part, part, ag_send.at[i], ag_recv.at[i], along(axis, k))

    def ag_start(number):
        for k in range(1, 4):
            ag_copy(number, k).start()

    def ag_land(number):
        for k in range(1, 4):
            ag_copy(number, k).wait_recv()

    def q1x_copy(k):
        return remote(q1x.at[x], q1x.at[x], q1x_send.at[k], q1x_recv.at[k], along("x", k))

    def q1_copy(k):
        part = q1.at[pl.ds(pl.multiple_of(chip * K, K), K)]
        return remote(part, part, q1_send.at[k], q1_recv.at[k], plane(k)[1])

    ag_start(0)
    ag_start(1)
    for k in range(1, 4):
        q1x_copy(k).start()
    ag_land(0)
    ag_start(2)
    ag_land(1)
    ag_start(3)
    for k in range(1, 4):
        q1x_copy(k).wait_recv()
    level_one = q1x[0].astype(F32) + q1x[1].astype(F32) + q1x[2].astype(F32) + q1x[3].astype(F32)
    q1[pl.ds(pl.multiple_of(chip * K, K), K), :] = level_one.astype(BF)

    def q1_start(k, carry):
        q1_copy(k).start()
        return carry

    lax.fori_loop(1, 16, q1_start, 0)
    ag_land(2)
    ag_start(4)
    ag_land(3)
    ag_start(5)

    @pl.when(has_before)
    def _():
        to_after_wait = remote(mine, win.at[pl.ds(0, 1024)], win_send.at[0], win_recv.at[0], after)
        to_after_wait.wait_recv()

    @pl.when(has_after)
    def _():
        to_before_wait = remote(mine, win.at[pl.ds(2048, 1024)], win_send.at[1], win_recv.at[1], before)
        to_before_wait.wait_recv()

    def window_coeffs(i, carry):
        rows = pl.ds(pl.multiple_of(i * P_SIZE, P_SIZE), P_SIZE)
        into = pl.ds(pl.multiple_of(i * K, K), K)
        cw[into, :] = dot(basis[i], win[rows, :]).astype(BF)
        return carry

    lax.fori_loop(0, 24, window_coeffs, 0)
    loads[1].wait()
    loads[2].wait()

    def leaf_far(i, carry):
        rows = pl.ds(pl.multiple_of(i * 128, 128), 128)
        part = dot(fl_mat[rows, :], cw[...])
        local_half[0, rows, :] = part[:, :HALF]
        local_half[1, rows, :] = part[:, HALF:]
        return carry

    lax.fori_loop(0, 4, leaf_far, 0)

    def near(i, carry):
        rows = pl.ds(pl.multiple_of(i * 128, 128), 128)
        w_ref[rows, :] = dot(c_mat[rows, :], win[...])
        return carry

    lax.fori_loop(0, 8, near, 0)

    loads[3].wait()
    loads[4].wait()
    ag_land(4)
    ag_land(5)

    def pick(j, carry):
        gathered[pl.ds(pl.multiple_of(j * K, K), K), :] = ag[idx_s[j]]
        return carry

    lax.fori_loop(0, 32, pick, 0)

    def far_copy(k):
        there, device = plane(k)
        return remote(far_out.at[there], far_in.at[k], far_send.at[k], far_recv.at[k], device)

    def far_step(k, carry):
        there, _ = plane(k)
        far_out[there] = dot(s_mat[there], gathered[...]).astype(BF)
        far_copy(k).start()
        return carry

    lax.fori_loop(1, 16, far_step, 0)

    def q1_land(k, carry):
        q1_copy(k).wait_recv()
        return carry

    lax.fori_loop(1, 16, q1_land, 0)
    own = dot(s_mat[chip], gathered[...]) + dot(falling_ref[...], q1[...])

    def far_sum(k, total):
        far_copy(k).wait_recv()
        return total + far_in[k].astype(F32)

    own = lax.fori_loop(1, 16, far_sum, own)
    l2[pl.ds(pl.multiple_of(chip * 128, 128), 128), :] = own.astype(BF)

    def l2_copy(k):
        part = l2.at[pl.ds(pl.multiple_of(chip * 128, 128), 128)]
        return remote(part, part, l2_send.at[k], l2_recv.at[k], plane(k)[1])

    def l2_start(k, carry):
        l2_copy(k).start()
        return carry

    lax.fori_loop(1, 16, l2_start, 0)

    def l2_land(k, carry):
        l2_copy(k).wait_recv()
        return carry

    lax.fori_loop(1, 16, l2_land, 0)

    def down_sibling(i, carry):
        rows = pl.ds(pl.multiple_of(512 + i * 128, 128), 128)
        into = pl.ds(pl.multiple_of(i * 128, 128), 128)
        sib_out[into, :] = dot(down_mat[rows, :], l2[...]).astype(BF)
        return carry

    lax.fori_loop(0, 4, down_sibling, 0)
    leaf_swap = remote(sib_out, sib_in, sib_send.at[1], sib_recv.at[1], sibling)
    leaf_swap.start()

    def down_own(i, carry):
        rows = pl.ds(pl.multiple_of(i * 128, 128), 128)
        merged[core, rows, :] = (local_half[core, rows, :] + dot(down_mat[rows, :], l2[...])).astype(BF)
        return carry

    lax.fori_loop(0, 4, down_own, 0)
    leaf_swap.wait_recv()
    merged[1 - core] = (local_half[1 - core] + sib_in[...].astype(F32)).astype(BF)

    def finish(i, carry):
        rows = pl.ds(pl.multiple_of(i * P_SIZE, P_SIZE), P_SIZE)
        part = pl.ds(pl.multiple_of(i * K, K), K)
        for h in range(2):
            lanes = pl.ds(h * HALF, HALF)
            value = w_ref[rows, lanes] + lax.dot_general(
                basis[8 + i], merged[h, part, :], (((0,), (0,)), ((), ())), preferred_element_type=F32
            )
            w_ref[rows, lanes] = value
            wb_ref[rows, lanes] = value.astype(BF)
        return carry

    lax.fori_loop(0, 8, finish, 0)

    coeff_swap.wait_send()
    leaf_swap.wait_send()

    @pl.when(has_after)
    def _():
        to_after.wait_send()

    @pl.when(has_before)
    def _():
        to_before.wait_send()

    for number in range(6):
        for k in range(1, 4):
            ag_copy(number, k).wait_send()
    for k in range(1, 4):
        q1x_copy(k).wait_send()

    def drain(k, carry):
        rs_copy(k).wait_send()
        q1_copy(k).wait_send()
        far_copy(k).wait_send()
        l2_copy(k).wait_send()
        return carry

    lax.fori_loop(1, 16, drain, 0)


def apply_operator(idx, v, basis, falling, c_mat, fl_mat, tv, s_mat, down):
    smem = pl.BlockSpec(memory_space=pltpu.SMEM)
    vmem = pl.BlockSpec(memory_space=pltpu.VMEM)
    anywhere = pl.BlockSpec(memory_space=pl.ANY)
    return pl.pallas_call(
        apply_kernel,
        out_shape=(
            jax.ShapeDtypeStruct((1024, 256), F32),
            jax.ShapeDtypeStruct((1024, 256), BF),
        ),
        in_specs=[smem, vmem, vmem, vmem] + [anywhere] * 5,
        out_specs=(vmem, vmem),
        scratch_shapes=[
            VMEM(c_mat.shape, BF),
            VMEM(fl_mat.shape, BF),
            VMEM(tv.shape, BF),
            VMEM(s_mat.shape, BF),
            VMEM(down.shape, BF),
            VMEM((3072, 256), BF),
            VMEM((1536, 256), BF),
            VMEM((2, 512, HALF), BF),
            VMEM((1024, HALF), BF),
            VMEM((2, 512, HALF), F32),
            VMEM((16, 192, HALF), BF),
            VMEM((16, 192, HALF), BF),
            VMEM((4, K, HALF), BF),
            VMEM((1024, HALF), BF),
            VMEM((128, K, HALF), BF),
            VMEM((2048, HALF), BF),
            VMEM((16, 128, HALF), BF),
            VMEM((16, 128, HALF), BF),
            VMEM((2048, HALF), BF),
            VMEM((512, HALF), BF),
            VMEM((512, HALF), BF),
            VMEM((2, 512, HALF), BF),
            DMA((5,)),
            DMA((2,)),
            DMA((2,)),
            DMA((2,)),
            DMA((2,)),
            DMA((16,)),
            DMA((16,)),
            DMA((4,)),
            DMA((4,)),
            DMA((16,)),
            DMA((16,)),
            DMA((18,)),
            DMA((18,)),
            DMA((16,)),
            DMA((16,)),
            DMA((16,)),
            DMA((16,)),
        ],
        compiler_params=pltpu.CompilerParams(
            collective_id=1, has_side_effects=True, vmem_limit_bytes=56 * 1024 * 1024
        ),
        name="apply_operator",
    )(idx, v, basis, falling, c_mat, fl_mat, tv, s_mat, down)


def least_squares(beta_norm, first_diag, first_below, second_top, second_diag, second_below):
    first_radius = jnp.sqrt(first_diag * first_diag + first_below * first_below)
    first_cos = first_diag / first_radius
    first_sin = first_below / first_radius
    upper_term = first_cos * second_top + first_sin * second_diag
    lower_term = first_cos * second_diag - first_sin * second_top
    second_radius = jnp.sqrt(lower_term * lower_term + second_below * second_below)
    second_cos = lower_term / second_radius
    second_sin = second_below / second_radius
    weight_two = -first_sin * beta_norm * second_cos / second_radius
    weight_one = (first_cos * beta_norm - upper_term * weight_two) / first_radius
    return (weight_one, weight_two, first_sin * second_sin * beta_norm)


def project(sums, sizes):
    pp, pa, aa, pb, ab, bb = sums
    size_p, size_a, size_b = sizes
    beta = jnp.sqrt(size_p * size_p * pp + EPS)
    scale_p, scale_a, scale_b = size_p / beta, size_a / beta, size_b / beta
    first_first = scale_p * scale_p * pp
    first_image = scale_p * scale_a * pa
    first_diag = first_image
    image_image = scale_a * scale_a * aa
    rest = image_image - first_diag * first_diag * (2.0 - first_first)
    first_below = jnp.sqrt(jnp.maximum(rest, 0.0) + EPS)
    inverse = 1.0 / first_below
    first_second = (first_image - first_diag * first_first) * inverse
    second_second = jnp.maximum(rest, 0.0) * inverse * inverse
    scale_two = scale_b * inverse
    diag_two = first_diag * inverse
    first_b = scale_p * scale_two * pb
    a_b = scale_a * scale_two * ab
    b_b = scale_two * scale_two * bb
    second_top = first_b - diag_two * first_image
    image_image_two = a_b - diag_two * image_image
    second_diag = (image_image_two - first_diag * second_top) * inverse
    square = b_b - 2.0 * diag_two * a_b + diag_two * diag_two * image_image
    rest_two = (
        square
        - second_top * second_top * (2.0 - first_first)
        - second_diag * second_diag * (2.0 - second_second)
        + 2.0 * second_top * second_diag * first_second
    )
    second_below = jnp.sqrt(jnp.maximum(rest_two, 0.0) + EPS)
    weight_one, weight_two, estimate = least_squares(
        beta, first_diag, first_below, second_top, second_diag, second_below
    )
    along_a = weight_two * inverse / beta
    along_p = weight_one / beta - along_a * first_diag
    return along_p, along_a, estimate


def finish_kernel(
    p_ref, w1_ref, w2_ref, panels_ref, pot_ref, out_ref, est_ref, high, low, w1_panel, part, box, send_sem, recv_sem
):
    x, z, y, core = place()

    def along(stage, k):
        if stage == 0:
            return (x, leaf_of(z, y, 1 - core))
        if stage == 1:
            return (lax.rem(x + k, 4), leaf_of(z, y, core))
        if stage == 2:
            return (x, leaf_of(z, lax.rem(y + k, 4), core))
        return (x, leaf_of(lax.rem(z + k, 4), y, core))

    peers = [(stage, k) for stage in range(4) for k in range(1, 2 if stage == 0 else 4)]
    coords = (core, x, y, z)

    barrier = pltpu.get_barrier_semaphore()
    for stage, k in peers:
        pl.semaphore_signal(barrier, inc=1, device_id=along(stage, k), device_id_type=MESH)

    def col_max(ref):
        return jnp.maximum(jnp.max(jnp.abs(ref[...]), axis=0, keepdims=True), 1e-30)

    size_p, size_a, size_b = col_max(p_ref), col_max(w1_ref), col_max(w2_ref)
    inv_p, inv_a, inv_b = 1.0 / size_p, 1.0 / size_a, 1.0 / size_b

    def add(i, carry):
        rows = pl.ds(pl.multiple_of(i * 32, 32), 32)
        p, a, b = p_ref[rows, :] * inv_p, w1_ref[rows, :] * inv_a, w2_ref[rows, :] * inv_b
        terms = (p * p, p * a, a * a, p * b, a * b, b * b)
        return tuple(c + jnp.sum(t.reshape(4, 8, 256), axis=0) for c, t in zip(carry, terms))

    sums = lax.fori_loop(0, 32, add, tuple(jnp.zeros((8, 256), F32) for _ in range(6)))
    sums = [jnp.sum(s, axis=0, keepdims=True) for s in sums]
    sizes = [size_p, size_a, size_b]

    pl.semaphore_wait(barrier, len(peers))

    pairs = ((0, 0), (0, 1), (1, 1), (0, 2), (1, 2), (2, 2))

    def copy(stage, k):
        i = stage * 4 + k
        return remote(
            box.at[stage, coords[stage]], box.at[stage, coords[stage]], send_sem.at[i], recv_sem.at[i], along(stage, k)
        )

    for stage in range(4):
        count = 2 if stage == 0 else 4
        for i in range(6):
            part[i : i + 1, :] = sums[i]
        for i in range(3):
            part[8 + i : 9 + i, :] = sizes[i]
        box[stage, coords[stage]] = part[...]
        for k in range(1, count):
            copy(stage, k).start()
        if stage == 0:
            value = w1_ref[...]
            top = value.astype(BF)
            high[...] = top
            low[...] = (value - top.astype(F32)).astype(BF)
        if stage in (1, 2):
            def unorder(i, carry):
                rows = pl.ds(pl.multiple_of(i * 128, 128), 128)
                wanted = lax.broadcasted_iota(jnp.int32, (128, 1024), 0) + i * 128
                hot = jnp.where(panels_ref[...] == wanted, 1.0, 0.0).astype(BF)
                w1_panel[rows, :] = dot(hot, high[...]) + dot(hot, low[...])
                return carry

            lax.fori_loop(4 * (stage - 1), 4 * stage, unorder, 0)
        for k in range(1, count):
            copy(stage, k).wait_recv()
        got = [box[stage, i] for i in range(count)]
        new_sizes = []
        for i in range(3):
            top_size = got[0][8 + i : 9 + i]
            for g in got[1:]:
                top_size = jnp.maximum(top_size, g[8 + i : 9 + i])
            new_sizes.append(top_size)
        factors = [[g[8 + i : 9 + i] / new_sizes[i] for i in range(3)] for g in got]
        sums = []
        for i, (a, b) in enumerate(pairs):
            value = got[0][i : i + 1] * (factors[0][a] * factors[0][b])
            for g, f in zip(got[1:], factors[1:]):
                value = value + g[i : i + 1] * (f[a] * f[b])
            sums.append(value)
        sizes = new_sizes

    along_p, along_a, estimate = project(sums, sizes)
    est_ref[...] = estimate

    def write(i, carry):
        rows = pl.ds(pl.multiple_of(i * 32, 32), 32)
        out_ref[rows, :] = along_p * pot_ref[rows, :] + along_a * w1_panel[rows, :]
        return carry

    lax.fori_loop(0, 32, write, 0)
    for stage, k in peers:
        copy(stage, k).wait_send()


def finish(p_slot, w1, w2, panels, potentials):
    vmem = pl.BlockSpec(memory_space=pltpu.VMEM)
    return pl.pallas_call(
        finish_kernel,
        out_shape=(jax.ShapeDtypeStruct((1024, 256), F32), jax.ShapeDtypeStruct((1, 256), F32)),
        in_specs=[vmem] * 5,
        out_specs=(vmem, vmem),
        scratch_shapes=[
            VMEM((1024, 256), BF),
            VMEM((1024, 256), BF),
            VMEM((1024, 256), F32),
            VMEM((16, 256), F32),
            VMEM((4, 4, 16, 256), F32),
            DMA((16,)),
            DMA((16,)),
        ],
        compiler_params=pltpu.CompilerParams(
            collective_id=2, has_side_effects=True, vmem_limit_bytes=40 * 1024 * 1024
        ),
        name="finish",
    )(p_slot, w1, w2, panels, potentials)


def on_device(
    potentials,
    leaf_panels,
    near_blocks,
    near_target,
    near_source,
    near_count,
    leaf_basis,
    far_leaf,
    far_leaf_target,
    far_leaf_source,
    leaf_transfer,
    leaf_parent,
    far_two,
    far_two_target,
    far_two_source,
    two_transfer,
    two_parent,
    far_one,
    far_one_target,
    far_one_source,
):
    group = lax.axis_index("grp")
    chip = lax.axis_index("leaf") // 2
    axes = ("grp", "leaf")

    swap = [(i, i ^ 1) for i in range(32)]
    numbers = jnp.concatenate([far_two_target[0], far_two_source[0], leaf_parent])
    matrices = jnp.concatenate([far_two, leaf_transfer], axis=0)
    other_numbers = lax.ppermute(numbers, "leaf", swap)
    other_matrices = lax.ppermute(matrices, "leaf", swap)
    basis_before = lax.ppermute(leaf_basis, axes, [(i, i + 1) for i in range(127)])
    basis_after = lax.ppermute(leaf_basis, axes, [(i + 1, i) for i in range(127)])

    c_mat, fl_mat = combine(
        near_target, near_source, near_count, far_leaf_target, far_leaf_source, near_blocks, far_leaf
    )

    high = potentials.astype(BF)
    low = (potentials - lax.reduce_precision(potentials, 8, 7)).astype(BF)
    slots = (leaf_panels[0][:, None] == jnp.arange(1024, dtype=jnp.int32)[None, :]).astype(BF)
    ordered = dot(slots, jnp.concatenate([high, low], axis=1))
    v0 = ordered[:, :256].astype(BF)
    p_slot = ordered[:, :256] + ordered[:, 256:]

    basis = jnp.concatenate([basis_before, leaf_basis, basis_after], axis=0)
    targets = jnp.concatenate([far_two_target[0], other_numbers[:16]])
    sources = jnp.concatenate([far_two_source[0], other_numbers[16:32]])
    parents = jnp.concatenate([leaf_parent, other_numbers[32:]])
    far_all = jnp.concatenate([far_two, other_matrices[:16]], axis=0)
    transfer = jnp.concatenate([leaf_transfer, other_matrices[16:]], axis=0)

    zero = jnp.zeros((), BF)
    clusters = jnp.arange(32, dtype=jnp.int32)
    parent_rows = jnp.repeat(parents, K)
    up = jnp.transpose(transfer, (2, 0, 1)).reshape(K, 1024)
    t2 = jnp.where(parent_rows[None, None, :] == clusters[:, None, None], up[None], zero)
    own_two = jnp.take(two_transfer, group * 32 + parents, axis=0)
    top_of = jnp.take(two_parent, group * 32 + parents)
    composite = jnp.einsum("lxb,lax->bla", own_two, transfer, preferred_element_type=F32)
    composite = composite.astype(BF).reshape(K, 1024)
    tops = jnp.arange(16, dtype=jnp.int32)
    v_up = jnp.where(jnp.repeat(top_of, K)[None, None, :] == tops[:, None, None], composite[None], zero)
    tv = jnp.concatenate([t2.reshape(16, 128, 1024), v_up], axis=1)

    down = jnp.where(
        parent_rows[:, None] == (jnp.arange(2048, dtype=jnp.int32) // K)[None, :],
        jnp.tile(transfer.reshape(1024, K), (1, 32)),
        zero,
    )

    far_flat = jnp.transpose(far_all, (1, 0, 2)).reshape(K, 2048)
    s_mat = jnp.where(
        jnp.repeat(targets, K)[None, None, :] == clusters[:, None, None], far_flat[None], zero
    ).reshape(16, 128, 2048)

    source_group, source_cluster = sources // 32, sources % 32
    source_chip, parity = source_cluster // 2, source_cluster % 2
    idx = jnp.where(
        parity == 0,
        source_chip * 4 + source_group,
        64 + ((source_chip % 4) * 4 + source_group) * 4 + source_chip // 4,
    )

    mine = group * 32 + chip * 2
    own_pair = lax.dynamic_slice_in_dim(two_transfer, mine, 2, 0)
    pair_top = lax.dynamic_slice_in_dim(two_parent, mine, 2, 0)
    pick = (far_one_target[None, None, :] == pair_top[:, None, None]) & (
        far_one_source[None, None, :] == tops[None, :, None]
    )
    rows_one = dot(pick.reshape(32, 32).astype(BF), far_one.reshape(32, K * K)).astype(BF)
    falling = jnp.einsum(
        "pax,pvxb->pavb", own_pair, rows_one.reshape(2, 16, K, K), preferred_element_type=F32
    )
    falling = falling.astype(BF).reshape(128, 1024)

    def operator(v):
        return apply_operator(idx, v, basis, falling, c_mat, fl_mat, tv, s_mat, down)

    w1, w1_short = operator(v0)
    w2, _ = operator(w1_short)
    solution_part, estimate = finish(p_slot, w1, w2, leaf_panels, potentials)
    return solution_part, estimate[0]


def solution(mesh):
    both = P(("grp", "leaf"))
    in_specs = (both,) * 15 + (P(),) * 5
    return jax.shard_map(
        on_device, mesh=mesh, in_specs=in_specs, out_specs=(both, P()), check_vma=False
    )
```

time: 1200 us -> 261 us (0.22)
  blocking collectives: 690 us -> 0 us
  waiting for transfers between devices: 192 us -> 0.01 us
  Pallas kernels: 0 us -> 189 us
  matrix products: 140 us -> 3.13 us
  local copies, waits for them, and re-layouts: 116 us -> 38.3 us
  between operations: 15.6 us -> 1.58 us
  other arithmetic: 34.1 us -> 22.1 us
    psum x8 -> x0, blocking collectives: 690 us -> none  [the longest x2 301 us: apply(): group_total = lax.psum(partial_value, 'leaf').astype(jnp.bfloat16)]
    pallas_call x0 -> x4, Pallas kernels: none -> 189 us  [the longest x2 148 us: apply_operator(): pl.pallas_call(apply_kernel, out_shape=(jax.ShapeDtypeStruct((1024, 256),...]
    psum x2 -> x0, waiting for transfers between devices: 172 us -> none  [apply(): level_two = (lax.psum(far_sum, 'leaf') + falling).astype(jnp.bfloat16)]
    dot_general x31 -> x4, matrix products: 140 us -> 3.13 us  [the longest x2 1.5 us: dot(): return jnp.dot(a, b, preferred_element_type=F32)]
    gather x12 -> x2, local copies, waits for them, and re-layouts: 40.3 us -> 2.85 us  [the longest x1 2.19 us: on_device(): own_two = jnp.take(two_transfer, group * 32 + parents, axis=0)]
    all_gather x2 -> x0, waiting for transfers between devices: 18.1 us -> none  [apply(): sources = lax.all_gather(group_total, 'grp', axis=0, tiled=True)]
    unnamed x112 -> x22, local copies, waits for them, and re-layouts: 30.8 us -> 14.6 us
    dot_general x1 -> x0, local copies, waits for them, and re-layouts: 15.9 us -> none  [on_device(): jnp.dot(pair_select, near_blocks.reshape(slot_total, P_SIZE * P_SIZE), pr...]
  transfers between devices with their start and end apart: 8 -> 4, of which waited for: 4 -> 0; matrix products, arithmetic and copies ran while one was open for 13% -> 14% of each run, Pallas kernels for 0% -> 10%
where the time goes in v1:
time: 261 us; the launch traced here: 260 us
  Pallas kernels  189 us (72%)
  local copies, waits for them, and re-layouts  38.3 us (15%)
  other arithmetic  22.1 us (8%)
  starting transfers between devices  5.62 us (2%)
  matrix products  3.13 us (1%)
    pallas_call x2, Pallas kernels, apply_operator(): pl.pallas_call(apply_kernel, out_shape=(jax.ShapeDtypeStruct((1024, 256),...  148 us
    pallas_call x1, Pallas kernels, combine(): pl.pallas_call(combine_kernel, grid=(NEAR_STEPS,), out_shape=(jax.ShapeDt...  27.2 us
    unnamed x22, local copies, waits for them, and re-layouts  14.6 us
    pallas_call x1, Pallas kernels, finish(): pl.pallas_call(finish_kernel, out_shape=(jax.ShapeDtypeStruct((1024, 256)...  13.6 us
    another operation x3, local copies, waits for them, and re-layouts, on_device(): jnp.tile(transfer.reshape(1024, K), (1, 32))  9.2 us
  transfers between devices with their start and end apart: 4, of which 0 were waited for; matrix products, arithmetic and copies ran while one was open for 14% of the time, Pallas kernels for 10%

profile of v1, /device:TPU:0, one launch (start us, length us, event | category | flops | bytes accessed | tf_op | source)
XLA Modules:
  0.0 259.7 jit_solution(13039003132756393677)
XLA Ops:
  0.6 2.0 collective-permute-start.1
  2.6 1.3 collective-permute-start.2
  3.9 1.3 pad_add_fusion
  5.2 2.4 collective-permute-start
  7.5 1.9 pad_maximum_fusion.1
  10.7 1.5 reshape.231
  13.9 1.3 reshape.232
  15.3 1.7 fusion.20
  17.0 1.3 fusion
  18.4 4.7 %copy.28 = bf16[128,64,64]{2,1,0:T(8,128)(2,1)} copy(bf16[128,64,64]{0,2,1:T(8,128)(2,1)} %param.35) | data formatting | bytes 2097152 | tf_op args[15]
  23.2 5.2 %copy.30.far_ref = bf16[192,64,64]{2,1,0:T(8,128)(2,1)} copy(bf16[192,64,64]{0,2,1:T(8,128)(2,1)} %param.27) | data formatting | bytes 3145728 | tf_op args[7]
  28.4 1.3 convolution_convert_fusion.1
  29.7 27.2 %combine.1 = (bf16[1024,3072]{1,0:T(8,128)(2,1)}, bf16[512,1536]{1,0:T(8,128)(2,1)}) custom-call(s32[1,384]{1,0:T(1,128)} %near_target.1, s32[1,384]{1,0:T(1,128)} %near_source.1, s32[1]{0:T(128)S(6)} %copy.42.near_count, s32[1,192]{1,0:T(1,128)} %far_target.1, s32[1,192]{1,0:T(1,128)} %far_source.1, bf16[384,128,128]{2,1,0:T(8,128)(2,1)} %near_ref.1, ...), custom_call_target="tpu_custom_call" | custom-call | flops 10000000 | bytes 20000000 | tf_op jit(solution)/shard_map/combine/pallas_call | solution.py:83
  64.1 2.2 gather_fusion.1
  66.3 1.3 compare_select_fusion.3.idx_s
  74.1 2.5 tile.11
  76.6 6.6 %copy.36 = bf16[1024,2048]{1,0:T(8,128)(2,1)} copy(bf16[1024,2048]{0,1:T(8,128)(2,1)} %bitcast.37) | data formatting | bytes 8388608 | tf_op jit(solution)/shard_map/tile | solution.py:800
  83.6 3.3 %pad_maximum_fusion.tv_hbm = bf16[16,192,1024]{2,1,0:T(8,128)(2,1)} fusion(bf16[16,64,1024]{2,1,0:T(8,128)(2,1)S(1)} %broadcast_select_fusion.2, bf16[16,128,1024]{2,1,0:T(8,128)(2,1)S(1)} %bitcast.36), kind=kLoop, calls=%fused_computation.4 | loop fusion | flops 12582912 | bytes 12582912 | tf_op jit(solution)/shard_map/concatenate | solution.py:796
  87.0 4.3 %compare_select_fusion.down_hbm = bf16[1024,2048]{1,0:T(8,128)(2,1)} fusion(bf16[1024,2048]{1,0:T(8,128)(2,1)} %copy.36, s32[2048]{0:T(1024)S(1)} %add_select_fusion, s32[1024]{0:T(1024)S(1)} %eq.143), kind=kLoop, calls=%fused_computation.2 | loop fusion | flops 4194304 | bytes 8400896 | tf_op jit(solution)/shard_map/jit(_where)/select_n | solution.py:798
  91.2 4.0 %broadcast_select_fusion = bf16[32,64,2048]{2,1,0:T(8,128)(2,1)} fusion(pred[32,2048]{1,0:T(8,128)(4,1)S(1)} %iota_compare_fusion.2, bf16[64,2048]{1,0:T(8,128)(2,1)S(1)} %broadcast_in_dim.114), kind=kLoop, calls=%fused_computation.3 | loop fusion | flops 4194304 | bytes 8716288 | tf_op jit(solution)/shard_map/jit(_where)/select_n | solution.py:805
  95.2 75.4 %apply_operator.2 = (f32[1024,256]{1,0:T(8,128)}, bf16[1024,256]{1,0:T(8,128)(2,1)}) custom-call(s32[32]{0:T(128)} %compare_select_fusion.3.idx_s, bf16[1024,256]{1,0:T(8,128)(2,1)} %slice.41.v_ref, bf16[24,64,128]{2,1,0:T(8,128)(2,1)} %copy-done.5, bf16[128,1024]{1,0:T(8,128)(2,1)} %reshape.233.falling_ref, bf16[1024,3072]{1,0:T(8,128)(2,1)} %get-tuple-element.9.c_hbm, ...), custom_call_target="tpu_custom_call" | custom-call | tf_op jit(solution)/shard_map/apply_operator/pallas_call | solution.py:501
  170.6 72.7 %apply_operator.3 = (f32[1024,256]{1,0:T(8,128)}, bf16[1024,256]{1,0:T(8,128)(2,1)}) custom-call(s32[32]{0:T(128)} %compare_select_fusion.3.idx_s, bf16[1024,256]{1,0:T(8,128)(2,1)} %get-tuple-element.12.v_ref, bf16[24,64,128]{2,1,0:T(8,128)(2,1)} %copy-done.5, bf16[128,1024]{1,0:T(8,128)(2,1)} %reshape.233.falling_ref, ...), custom_call_target="tpu_custom_call" | custom-call | tf_op jit(solution)/shard_map/apply_operator/pallas_call | solution.py:501
  243.4 1.2 copy-done.2
  244.6 13.6 %finish.1 = (f32[1024,256]{1,0:T(8,128)S(1)}, f32[1,256]{1,0:T(1,128)S(1)}) custom-call(f32[1024,256]{1,0:T(8,128)S(1)} %slice_add_fusion.p_ref, f32[1024,256]{1,0:T(8,128)S(1)} %copy-done.1, f32[1024,256]{1,0:T(8,128)S(1)} %copy-done.2, s32[1,1024]{1,0:T(1,128)S(1)} %copy-done.3, f32[1024,256]{1,0:T(8,128)S(1)} %copy-done), custom_call_target="tpu_custom_call" | custom-call | tf_op jit(solution)/shard_map/finish/pallas_call | solution.py:712
  (63 shorter events, 18.0 us)
Async XLA Ops:
  0.6 16.4 %copy-start.3 = (s32[1,1024]{1,0:T(1,128)S(1)}, s32[1,1024]{1,0:T(1,128)}, u32[]{:S(2)}) copy-start(s32[1,1024]{1,0:T(1,128)} %panels_ref.1) | copy-start | bytes 12292
  0.6 66.9 %collective-permute-start.1 = (bf16[8,64,128]{2,1,0:T(8,128)(2,1)}, bf16[8,64,128]{2,1,0:T(8,128)(2,1)}, u32[]{:S(2)}, u32[]{:S(2)}) collective-permute-start(bf16[8,64,128]{2,1,0:T(8,128)(2,1)} %param.26), channel_id=1, source_target_pairs={{0,1},{1,2},{2,3},{3,4},{4,5},{5,6},{6,7},{7,8},{8,9},{9,10},{10,1... | collective-permute-start | bytes 393224 | tf_op jit(solution)/shard_map/ppermute | solution.py:764
  2.6 66.8 %collective-permute-start.2 = (bf16[8,64,128]{2,1,0:T(8,128)(2,1)}, bf16[8,64,128]{2,1,0:T(8,128)(2,1)}, u32[]{:S(2)}, u32[]{:S(2)}) collective-permute-start(bf16[8,64,128]{2,1,0:T(8,128)(2,1)} %param.26), channel_id=1, source_target_pairs={{1,0},{2,1},{3,2},{4,3},{5,4},{6,5},{7,6},{8,7},{9,8},{10,9},{11,1... | collective-permute-start | bytes 393224 | tf_op jit(solution)/shard_map/ppermute | solution.py:765
  5.2 54.1 %collective-permute-start = (s32[40]{0:T(128)}, s32[40]{0:T(128)}, u32[]{:S(2)}, u32[]{:S(2)}) collective-permute-start(s32[40]{0:T(128)} %pad_add_fusion), channel_id=1, source_target_pairs={{0,1},{1,0},{2,3},{3,2},{4,5},{5,4},{6,7},{7,6},{8,9},{9,8},{10,11... | collective-permute-start | bytes 488 | tf_op jit(solution)/shard_map/ppermute | solution.py:762
  9.4 60.9 %collective-permute-start.3 = (bf16[24,64,64]{2,1,0:T(8,128)(2,1)}, bf16[24,64,64]{2,1,0:T(8,128)(2,1)}, u32[]{:S(2)}, u32[]{:S(2)}) collective-permute-start(bf16[24,64,64]{2,1,0:T(8,128)(2,1)} %pad_maximum_fusion.1), channel_id=1, source_target_pairs={{0,1},{1,0},{2,3},{3,2},{4,5},{5,4},{6,7},{7,6},{8,9},{9,8},{10,11... | collective-permute-start | bytes 589832 | tf_op jit(solution)/shard_map/ppermute | solution.py:763
  29.7 32.4 %copy-start.4 = (s32[128]{0:T(128)S(1)}, s32[128]{0:T(128)}, u32[]{:S(2)}) copy-start(s32[128]{0:T(128)} %param.36) | copy-start | bytes 1540
  57.0 14.4 %copy-start.7 = (bf16[8,64,64]{2,1,0:T(8,128)(2,1)S(1)}, bf16[8,64,64]{2,1,0:T(8,128)(2,1)}, u32[]{:S(2)}) copy-start(bf16[8,64,64]{2,1,0:T(8,128)(2,1)} %param.30) | copy-start | bytes 196612
  57.0 15.8 %copy-start.6 = (bf16[16,64,64]{2,1,0:T(8,128)(2,1)S(1)}, bf16[16,64,64]{2,1,0:T(8,128)(2,1)}, u32[]{:S(2)}) copy-start(bf16[16,64,64]{2,1,0:T(8,128)(2,1)} %param.32) | copy-start | bytes 393220
  70.3 6.3 %copy-start.5 = (bf16[24,64,128]{2,1,0:T(8,128)(2,1)}, bf16[24,64,128]{2,1,0:T(8,128)(2,1)S(1)}, u32[]{:S(2)}) copy-start(bf16[24,64,128]{2,1,0:T(8,128)(2,1)S(1)} %constant_dynamic-update-slice_fusion.basis) | copy-start | bytes 1179652
  170.6 72.8 %copy-start = (f32[1024,256]{1,0:T(8,128)S(1)}, f32[1024,256]{1,0:T(8,128)}, u32[]{:S(2)}) copy-start(f32[1024,256]{1,0:T(8,128)} %pot_ref.1) | copy-start | bytes 3145732
  170.6 72.8 %copy-start.1 = (f32[1024,256]{1,0:T(8,128)S(1)}, f32[1024,256]{1,0:T(8,128)}, u32[]{:S(2)}) copy-start(f32[1024,256]{1,0:T(8,128)} %get-tuple-element.11.w1_ref) | copy-start | bytes 3145732
  243.4 1.2 copy-start.2

commit v2 on v0

v2 whole, which is shorter than its diff:
```python
import jax
import jax.numpy as jnp
from jax import lax
from jax.experimental import pallas as pl
from jax.experimental.pallas import tpu as pltpu
from jax.sharding import PartitionSpec as P

P_SIZE = 128
K = 64
HALF = 128
EPS = 1e-06
BF = jnp.bfloat16
F32 = jnp.float32
MESH = pl.DeviceIdType.MESH
VMEM = pltpu.VMEM
DMA = pltpu.SemaphoreType.DMA
NEAR_STEPS = 8


def dot(a, b):
    return jnp.dot(a, b, preferred_element_type=F32)


def combine_kernel(
    near_target, near_source, near_count, far_target, far_source, near_ref, far_ref, c_ref, fl_ref, acc, facc
):
    step = pl.program_id(0)
    per_step = near_ref.shape[0]
    window = 24

    @pl.when(step == 0)
    def _():
        def zero(i, carry):
            acc[i] = jnp.zeros((P_SIZE, P_SIZE), F32)
            facc[i] = jnp.zeros((K, K), F32)
            return carry

        lax.fori_loop(0, acc.shape[0], zero, 0, unroll=8)

    live = jnp.clip(near_count[0] - step * per_step, 0, per_step)

    def add(j, carry):
        slot = step * per_step + j
        key = near_target[0, slot] * window + near_source[0, slot]
        acc[key] = acc[key] + near_ref[j].astype(F32)
        return carry

    lax.fori_loop(0, live, add, 0)

    @pl.when(step == pl.num_programs(0) - 1)
    def _():
        def add_far(j, carry):
            key = far_target[0, j] * window + far_source[0, j]
            facc[key] = facc[key] + far_ref[j].astype(F32)
            return carry

        lax.fori_loop(0, far_ref.shape[0], add_far, 0, unroll=4)

        def write(i, carry):
            t, s = i // window, i % window
            rows = pl.ds(pl.multiple_of(t * P_SIZE, P_SIZE), P_SIZE)
            lanes = pl.ds(pl.multiple_of(s * P_SIZE, P_SIZE), P_SIZE)
            c_ref[rows, lanes] = acc[i].astype(BF)
            return carry

        lax.fori_loop(0, acc.shape[0], write, 0, unroll=8)

        def write_far(i, carry):
            t, s = i // (window // 2), i % (window // 2)
            rows = pl.ds(pl.multiple_of(t * K, K), K)
            lanes = pl.ds(pl.multiple_of(s * 2 * K, 2 * K), 2 * K)
            both = jnp.concatenate([facc[2 * i], facc[2 * i + 1]], axis=1)
            fl_ref[rows, lanes] = both.astype(BF)
            return carry

        lax.fori_loop(0, facc.shape[0] // 2, write_far, 0, unroll=8)


def combine(near_target, near_source, near_count, far_target, far_source, near_blocks, far_leaf):
    smem = pl.BlockSpec(memory_space=pltpu.SMEM)
    slots = near_blocks.shape[0]
    per_step = slots // NEAR_STEPS
    return pl.pallas_call(
        combine_kernel,
        grid=(NEAR_STEPS,),
        out_shape=(
            jax.ShapeDtypeStruct((1024, 3072), BF),
            jax.ShapeDtypeStruct((512, 1536), BF),
        ),
        in_specs=[smem] * 5
        + [
            pl.BlockSpec((per_step, P_SIZE, P_SIZE), lambda i: (i, 0, 0)),
            pl.BlockSpec(far_leaf.shape, lambda i: (0, 0, 0)),
        ],
        out_specs=(
            pl.BlockSpec((1024, 3072), lambda i: (0, 0)),
            pl.BlockSpec((512, 1536), lambda i: (0, 0)),
        ),
        scratch_shapes=[VMEM((192, P_SIZE, P_SIZE), F32), VMEM((192, K, K), F32)],
        compiler_params=pltpu.CompilerParams(
            vmem_limit_bytes=56 * 1024 * 1024, dimension_semantics=("arbitrary",)
        ),
        cost_estimate=pl.CostEstimate(flops=10**7, bytes_accessed=20 * 10**6, transcendentals=0),
        name="combine",
    )(near_target, near_source, near_count, far_target, far_source, near_blocks, far_leaf)


def remote(src, dst, send, recv, device):
    return pltpu.make_async_remote_copy(
        src_ref=src, dst_ref=dst, send_sem=send, recv_sem=recv, device_id=device, device_id_type=MESH
    )


def place():
    x = lax.axis_index("grp")
    leaf = lax.axis_index("leaf")
    core = lax.rem(leaf, 2)
    chip = lax.div(leaf, 2)
    return x, lax.div(chip, 4), lax.rem(chip, 4), core


def leaf_of(z, y, core):
    return (z * 4 + y) * 2 + core


def loop(start, stop, body, unroll=1):
    def step(i, carry):
        body(i)
        return carry

    lax.fori_loop(start, stop, step, 0, unroll=unroll)


def rows_at(i, size):
    return pl.ds(pl.multiple_of(i * size, size), size)


BUFFERS = dict(
    c_mat=VMEM((1024, 3072), BF),
    fl_mat=VMEM((512, 1536), BF),
    tv_mat=VMEM((16, 192, 1024), BF),
    s_mat=VMEM((16, 128, 2048), BF),
    down_mat=VMEM((1024, 2048), BF),
    top_mat=VMEM((128, 2048), BF),
    up=VMEM((K, 1024), BF),
    composite=VMEM((K, 1024), BF),
    far_flat=VMEM((K, 2048), BF),
    transfer=VMEM((16, K, K), BF),
    far_all=VMEM((32, K, K), BF),
    basis=VMEM((24, K, P_SIZE), BF),
    other_numbers=VMEM((8, 128), jnp.int32),
    other_s=pltpu.SMEM((8, 128), jnp.int32),
    v0=VMEM((1024, 256), BF),
    p_slot=VMEM((1024, 256), F32),
    w1=VMEM((1024, 256), F32),
    w2=VMEM((1024, 256), F32),
    high=VMEM((1024, 512), BF),
    w1_panel=VMEM((1024, 256), F32),
    part=VMEM((16, 256), F32),
    box=VMEM((4, 4, 16, 256), F32),
    win=VMEM((2, 3072, 256), BF),
    cw=VMEM((1536, 256), BF),
    chalf=VMEM((2, 512, HALF), BF),
    c2=VMEM((2, 1024, HALF), BF),
    local_half=VMEM((2, 512, HALF), F32),
    rs_out=VMEM((16, 192, HALF), BF),
    rs_in=VMEM((2, 16, 192, HALF), BF),
    q1x=VMEM((2, 4, K, HALF), BF),
    q1=VMEM((2, 16, K, HALF), BF),
    ag0=VMEM((2, 64, 48, HALF), BF),
    ag1=VMEM((2, 64, 48, HALF), BF),
    ag2=VMEM((2, 64, 32, HALF), BF),
    q_two=VMEM((128, K, HALF), BF),
    gathered=VMEM((2048, HALF), BF),
    far_out=VMEM((16, 128, HALF), BF),
    far_in=VMEM((2, 16, 128, HALF), BF),
    l2=VMEM((2, 2048, HALF), BF),
    sib_out=VMEM((512, HALF), BF),
    sib_in=VMEM((2, 512, HALF), BF),
    merged=VMEM((2, 512, HALF), BF),
    load_sem=DMA((3,)),
    ex_send=DMA((5,)),
    ex_recv=DMA((5,)),
    win_send=DMA((2, 2)),
    win_recv=DMA((2, 2)),
    sib_send=DMA((2, 2)),
    sib_recv=DMA((2, 2)),
    rs_send=DMA((2, 16)),
    rs_recv=DMA((2, 16)),
    q1x_send=DMA((2, 4)),
    q1x_recv=DMA((2, 4)),
    q1_send=DMA((2, 16)),
    q1_recv=DMA((2, 16)),
    ag_send=DMA((2, 27)),
    ag_recv=DMA((2, 27)),
    far_send=DMA((2, 16)),
    far_recv=DMA((2, 16)),
    l2_send=DMA((2, 16)),
    l2_recv=DMA((2, 16)),
    sum_send=DMA((16,)),
    sum_recv=DMA((16,)),
)
NAMES = tuple(BUFFERS)


def steps_kernel(
    numbers_s,
    one_target_s,
    one_source_s,
    numbers_ref,
    panels_row,
    panels_col,
    pot_ref,
    basis_ref,
    transfer_ref,
    far_ref,
    two_ref,
    one_ref,
    c_hbm,
    fl_hbm,
    out_ref,
    est_ref,
    *scratch,
):
    b = dict(zip(NAMES, scratch))
    basis, transfer, far_all, other_s = b["basis"], b["transfer"], b["far_all"], b["other_s"]
    up, composite, far_flat = b["up"], b["composite"], b["far_flat"]
    tv_mat, s_mat, down_mat, top_mat = b["tv_mat"], b["s_mat"], b["down_mat"], b["top_mat"]
    x, z, y, core = place()
    chip = z * 4 + y
    me = x * 32 + chip * 2 + core

    loads = [
        pltpu.make_async_copy(c_hbm, b["c_mat"], b["load_sem"].at[0]),
        pltpu.make_async_copy(fl_hbm, b["fl_mat"], b["load_sem"].at[1]),
    ]
    for load in loads:
        load.start()

    sibling = (x, chip * 2 + 1 - core)
    before = (lax.rem(lax.div(me + 127, 32), 4), lax.rem(me + 31, 32))
    after = (lax.rem(lax.div(me + 1, 32), 4), lax.rem(me + 1, 32))
    has_before = me > 0
    has_after = me < 127

    def plane(k):
        tz = lax.rem(z + lax.div(k, 4), 4)
        ty = lax.rem(y + lax.rem(k, 4), 4)
        return tz * 4 + ty, (x, leaf_of(tz, ty, core))

    def along(axis, k):
        if axis == "x":
            return (lax.rem(x + k, 4), leaf_of(z, y, core))
        if axis == "y":
            return (x, leaf_of(z, lax.rem(y + k, 4), core))
        if axis == "z":
            return (x, leaf_of(lax.rem(z + k, 4), y, core))
        return sibling

    barrier = pltpu.get_barrier_semaphore()

    def greet(k):
        pl.semaphore_signal(barrier, inc=1, device_id=plane(k)[1], device_id_type=MESH)

    loop(1, 16, greet)
    for k in range(1, 4):
        pl.semaphore_signal(barrier, inc=1, device_id=along("x", k), device_id_type=MESH)
    pl.semaphore_signal(barrier, inc=1, device_id=sibling, device_id_type=MESH)

    @pl.when(has_before)
    def _():
        pl.semaphore_signal(barrier, inc=1, device_id=before, device_id_type=MESH)

    @pl.when(has_after)
    def _():
        pl.semaphore_signal(barrier, inc=1, device_id=after, device_id_type=MESH)

    high = b["high"]

    def split(i):
        rows = rows_at(i, 128)
        value = pot_ref[rows, :]
        top = value.astype(BF)
        high[rows, pl.ds(0, 256)] = top
        high[rows, pl.ds(256, 256)] = (value - top.astype(F32)).astype(BF)

    loop(0, 8, split)

    def order(i):
        rows = rows_at(i, 128)
        wanted = lax.broadcasted_iota(jnp.int32, (128, 1024), 1)
        hot = jnp.where(panels_col[rows, :] == wanted, 1.0, 0.0).astype(BF)
        value = dot(hot, high[...])
        b["v0"][rows, :] = value[:, :256].astype(BF)
        b["p_slot"][rows, :] = value[:, :256] + value[:, 256:]

    loop(0, 8, order)
    basis[pl.ds(8, 8)] = basis_ref[...]
    transfer[pl.ds(0, 8)] = transfer_ref[...]
    far_all[pl.ds(0, 16)] = far_ref[...]

    for it in range(2):

        @pl.when(jnp.logical_not(has_before))
        def _():
            b["win"][it, pl.ds(0, 1024), :] = jnp.zeros((1024, 256), BF)

        @pl.when(jnp.logical_not(has_after))
        def _():
            b["win"][it, pl.ds(2048, 1024), :] = jnp.zeros((1024, 256), BF)

    @pl.when(jnp.logical_not(has_before))
    def _():
        basis[pl.ds(0, 8)] = jnp.zeros((8, K, P_SIZE), BF)

    @pl.when(jnp.logical_not(has_after))
    def _():
        basis[pl.ds(16, 8)] = jnp.zeros((8, K, P_SIZE), BF)

    pl.semaphore_wait(barrier, 19 + has_before.astype(jnp.int32) + has_after.astype(jnp.int32))

    ex_send, ex_recv = b["ex_send"], b["ex_recv"]
    swaps = [
        remote(numbers_ref, b["other_numbers"], ex_send.at[0], ex_recv.at[0], sibling),
        remote(transfer_ref, transfer.at[pl.ds(8, 8)], ex_send.at[1], ex_recv.at[1], sibling),
        remote(far_ref, far_all.at[pl.ds(16, 16)], ex_send.at[2], ex_recv.at[2], sibling),
    ]
    for swap in swaps:
        swap.start()
    basis_after = remote(basis_ref, basis.at[pl.ds(0, 8)], ex_send.at[3], ex_recv.at[3], after)
    basis_before = remote(basis_ref, basis.at[pl.ds(16, 8)], ex_send.at[4], ex_recv.at[4], before)

    @pl.when(has_after)
    def _():
        basis_after.start()

    @pl.when(has_before)
    def _():
        basis_before.start()

    def number(row, i, count):
        return numbers_s[row, i] if i < count else other_s[row, i - count]

    def spread(values, lanes):
        index = lax.broadcasted_iota(jnp.int32, (1, lanes), 1) // K
        found = jnp.zeros((1, lanes), jnp.int32)
        for i, value in enumerate(values):
            found = jnp.where(index == i, value, found)
        return found

    def chosen(found, value):
        return jnp.where(found == value, 1.0, 0.0).astype(BF)

    def build_up():
        for swap in swaps[:2]:
            swap.wait_recv()
        fetch = pltpu.make_async_copy(b["other_numbers"], other_s, b["load_sem"].at[2])
        fetch.start()
        fetch.wait()
        parents = [number(2, l, 8) for l in range(16)]
        for i in range(8):
            lanes = pl.ds(i * 128, 128)
            pair = transfer[pl.ds(2 * i, 2)].reshape(128, K)
            up[:, lanes] = pair.astype(F32).T.astype(BF)
            both = [dot(transfer[2 * i + h], two_ref[parents[2 * i + h]]) for h in range(2)]
            composite[:, lanes] = jnp.concatenate(both, axis=0).T.astype(BF)
        parent_lanes = spread(parents, 1024)
        top_lanes = spread([numbers_s[3, parent] for parent in parents], 1024)

        def build(c):
            tv_mat[c // 2, rows_at(c % 2, K), :] = up[...] * chosen(parent_lanes, c)

        loop(0, 32, build)

        def build_top(u):
            tv_mat[u, pl.ds(128, K), :] = composite[...] * chosen(top_lanes, u)

        loop(0, 16, build_top)

    def build_rest():
        swaps[2].wait_recv()
        targets = [number(0, j, 16) for j in range(32)]
        for i in range(16):
            far_flat[:, pl.ds(i * 128, 128)] = jnp.concatenate([far_all[2 * i], far_all[2 * i + 1]], axis=1)
        target_lanes = spread(targets, 2048)

        def build_far(c):
            s_mat[c // 2, rows_at(c % 2, K), :] = far_flat[...] * chosen(target_lanes, c)

        loop(0, 32, build_far)

        for l in range(16):
            pair = jnp.concatenate([transfer[l], transfer[l]], axis=1)
            half = lax.broadcasted_iota(jnp.int32, (1, 128), 1) // K
            parent = number(2, l, 8)

            def build_down(i, l=l, pair=pair, half=half, parent=parent):
                down_mat[pl.ds(l * K, K), rows_at(i, 128)] = pair * chosen(half + 2 * i, parent)

            loop(0, 16, build_down, 4)

        one_lanes = spread([one_target_s[j] for j in range(32)], 2048)
        for i in range(16):
            far_flat[:, pl.ds(i * 128, 128)] = jnp.concatenate([one_ref[2 * i], one_ref[2 * i + 1]], axis=1)
        for h in range(2):
            wanted = numbers_s[3, chip * 2 + h]
            top_mat[pl.ds(h * K, K), :] = far_flat[...] * chosen(one_lanes, wanted)

    def apply(it, v, w, wb, beside_rs, beside_far):
        win, chalf, c2 = b["win"].at[it], b["chalf"], b["c2"].at[it]
        local_half, cw = b["local_half"], b["cw"]
        rs_out, rs_in, q1x, q1 = b["rs_out"], b["rs_in"].at[it], b["q1x"].at[it], b["q1"].at[it]
        ag = [b["ag0"].at[it], b["ag1"].at[it], b["ag2"].at[it]]
        q_two, gathered = b["q_two"], b["gathered"]
        far_out, far_in, l2 = b["far_out"], b["far_in"].at[it], b["l2"].at[it]
        sib_out, sib_in, merged = b["sib_out"], b["sib_in"].at[it], b["merged"]

        to_after = remote(v, win.at[pl.ds(0, 1024)], b["win_send"].at[it, 0], b["win_recv"].at[it, 0], after)
        to_before = remote(v, win.at[pl.ds(2048, 1024)], b["win_send"].at[it, 1], b["win_recv"].at[it, 1], before)

        def own_coeffs(i):
            part = dot(basis[8 + i], v[rows_at(i, P_SIZE), :]).astype(BF)
            chalf[0, rows_at(i, K), :] = part[:, :HALF]
            chalf[1, rows_at(i, K), :] = part[:, HALF:]

        loop(0, 8, own_coeffs, 8)
        coeff_swap = remote(
            chalf.at[1 - core], c2.at[pl.ds(512, 512)], b["sib_send"].at[it, 0], b["sib_recv"].at[it, 0], sibling
        )
        coeff_swap.start()

        @pl.when(has_after)
        def _():
            to_after.start()

        @pl.when(has_before)
        def _():
            to_before.start()

        c2[pl.ds(0, 512), :] = chalf[core]
        win[pl.ds(1024, 1024), :] = v[...]
        if it == 0:
            build_up()
        coeff_swap.wait_recv()

        def rs_copy(k):
            there, device = plane(k)
            return remote(rs_out.at[there], rs_in.at[k], b["rs_send"].at[it, k], b["rs_recv"].at[it, k], device)

        def rs_step(k):
            there, _ = plane(k)
            rs_out[there] = dot(tv_mat[there], c2[...]).astype(BF)
            rs_copy(k).start()

        loop(1, 16, rs_step)
        rs_in[0] = dot(tv_mat[chip], c2[...]).astype(BF)
        beside_rs()

        def rs_sum(k, total):
            rs_copy(k).wait_recv()
            return total + rs_in[k].astype(F32)

        total = lax.fori_loop(1, 16, rs_sum, rs_in[0].astype(F32)).astype(BF)

        homes = ((z * 4 + y) * 4 + x, (x * 4 + z) * 4 + y, (y * 4 + x) * 4 + z)
        orders = (("x", "y", "z"), ("y", "z", "x"), ("z", "x", "y"))
        lasts = (z, x, y)
        ag[0][homes[0]] = total[0:48]
        ag[1][homes[1]] = total[48:96]
        ag[2][homes[2]] = total[96:128]
        q1x[x] = total[128:192]

        def ag_copy(stream, stage, k):
            if stage == 0:
                first, count = homes[stream], 1
            elif stage == 1:
                first, count = lax.div(homes[stream], 4) * 4, 4
            else:
                first, count = lasts[stream] * 16, 16
            part = ag[stream].at[pl.ds(first, count)]
            i = (stream * 3 + stage) * 3 + k - 1
            return remote(
                part, part, b["ag_send"].at[it, i], b["ag_recv"].at[it, i], along(orders[stream][stage], k)
            )

        def ag_start(stream, stage):
            for k in range(1, 4):
                ag_copy(stream, stage, k).start()

        def ag_land(stream, stage):
            for k in range(1, 4):
                ag_copy(stream, stage, k).wait_recv()

        def q1x_copy(k):
            return remote(q1x.at[x], q1x.at[x], b["q1x_send"].at[it, k], b["q1x_recv"].at[it, k], along("x", k))

        def q1_copy(k):
            part = q1.at[chip]
            return remote(part, part, b["q1_send"].at[it, k], b["q1_recv"].at[it, k], plane(k)[1])

        for stream in range(3):
            ag_start(stream, 0)
        for k in range(1, 4):
            q1x_copy(k).start()
        for stream in range(3):
            ag_land(stream, 0)
            ag_start(stream, 1)
        for k in range(1, 4):
            q1x_copy(k).wait_recv()
        level_one = q1x[0].astype(F32) + q1x[1].astype(F32) + q1x[2].astype(F32) + q1x[3].astype(F32)
        q1[chip] = level_one.astype(BF)

        def q1_start(k):
            q1_copy(k).start()

        for stream in range(3):
            ag_land(stream, 1)
            ag_start(stream, 2)
        loop(1, 16, q1_start)

        @pl.when(has_before)
        def _():
            to_after.wait_recv()
            if it == 0:
                basis_after.wait_recv()

        @pl.when(has_after)
        def _():
            to_before.wait_recv()
            if it == 0:
                basis_before.wait_recv()

        def window_coeffs(i):
            cw[rows_at(i, K), :] = dot(basis[i], win[rows_at(i, P_SIZE), :]).astype(BF)

        loop(0, 24, window_coeffs, 4)
        if it == 0:
            for load in loads:
                load.wait()

        def leaf_far(i):
            part = dot(b["fl_mat"][rows_at(i, 128), :], cw[...])
            local_half[0, rows_at(i, 128), :] = part[:, :HALF]
            local_half[1, rows_at(i, 128), :] = part[:, HALF:]

        loop(0, 4, leaf_far)

        def near(i):
            w[rows_at(i, 128), :] = dot(b["c_mat"][rows_at(i, 128), :], win[...])

        loop(0, 8, near)

        for stream in range(3):
            ag_land(stream, 2)

        def join(i):
            ip, g = i // 4, i % 4
            iz, iy = ip // 4, ip % 4
            first, second, third = ag[0][i], ag[1][(g * 4 + iz) * 4 + iy], ag[2][(iy * 4 + g) * 4 + iz]
            q_two[g * 32 + 2 * ip] = jnp.concatenate([first, second[0:16]], axis=0)
            q_two[g * 32 + 2 * ip + 1] = jnp.concatenate([second[16:48], third], axis=0)

        loop(0, 64, join, 4)

        for j in range(32):
            gathered[pl.ds(j * K, K), :] = q_two[number(1, j, 16)]

        def far_copy(k):
            there, device = plane(k)
            return remote(far_out.at[there], far_in.at[k], b["far_send"].at[it, k], b["far_recv"].at[it, k], device)

        def far_step(k):
            there, _ = plane(k)
            far_out[there] = dot(s_mat[there], gathered[...]).astype(BF)
            far_copy(k).start()

        loop(1, 16, far_step)
        own = dot(s_mat[chip], gathered[...])

        def q1_land(k):
            q1_copy(k).wait_recv()

        loop(1, 16, q1_land)
        for j in range(32):
            gathered[pl.ds(j * K, K), :] = q1[one_source_s[j]]
        l_one = dot(top_mat[...], gathered[...]).astype(BF)
        falling = [dot(two_ref[chip * 2 + h], l_one[h * K : (h + 1) * K]) for h in range(2)]
        own = own + jnp.concatenate(falling, axis=0)
        beside_far()

        def far_sum(k, total):
            far_copy(k).wait_recv()
            return total + far_in[k].astype(F32)

        own = lax.fori_loop(1, 16, far_sum, own)
        l2[rows_at(chip, 128), :] = own.astype(BF)

        def l2_copy(k):
            part = l2.at[rows_at(chip, 128)]
            return remote(part, part, b["l2_send"].at[it, k], b["l2_recv"].at[it, k], plane(k)[1])

        def l2_start(k):
            l2_copy(k).start()

        loop(1, 16, l2_start)

        def drain(k):
            rs_copy(k).wait_send()
            q1_copy(k).wait_send()
            far_copy(k).wait_send()

        loop(1, 16, drain)
        coeff_swap.wait_send()
        for stream in range(3):
            for stage in range(3):
                for k in range(1, 4):
                    ag_copy(stream, stage, k).wait_send()
        for k in range(1, 4):
            q1x_copy(k).wait_send()

        @pl.when(has_after)
        def _():
            to_after.wait_send()

        @pl.when(has_before)
        def _():
            to_before.wait_send()

        def l2_land(k):
            l2_copy(k).wait_recv()

        loop(1, 16, l2_land)

        def down_sibling(i):
            sib_out[rows_at(i, 128), :] = dot(down_mat[rows_at(i + 4, 128), :], l2[...]).astype(BF)

        loop(0, 4, down_sibling)
        leaf_swap = remote(sib_out, sib_in, b["sib_send"].at[it, 1], b["sib_recv"].at[it, 1], sibling)
        leaf_swap.start()

        def down_own(i):
            rows = rows_at(i, 128)
            merged[core, rows, :] = (local_half[core, rows, :] + dot(down_mat[rows, :], l2[...])).astype(BF)

        loop(0, 4, down_own)
        leaf_swap.wait_recv()
        merged[1 - core] = (local_half[1 - core] + sib_in[...].astype(F32)).astype(BF)

        def finish(i):
            rows = rows_at(i, P_SIZE)
            for h in range(2):
                lanes = pl.ds(h * HALF, HALF)
                value = w[rows, lanes] + lax.dot_general(
                    basis[8 + i],
                    merged[h, rows_at(i, K), :],
                    (((0,), (0,)), ((), ())),
                    preferred_element_type=F32,
                )
                w[rows, lanes] = value
                if wb is not None:
                    wb[rows, lanes] = value.astype(BF)

        loop(0, 8, finish, 2)
        leaf_swap.wait_send()

        def l2_sent(k):
            l2_copy(k).wait_send()

        loop(1, 16, l2_sent)

    p_slot, w1, w2, w1_panel = b["p_slot"], b["w1"], b["w2"], b["w1_panel"]

    def unorder():
        def split_image(i):
            rows = rows_at(i, 128)
            value = w1[rows, :]
            top = value.astype(BF)
            high[rows, pl.ds(0, 256)] = top
            high[rows, pl.ds(256, 256)] = (value - top.astype(F32)).astype(BF)

        loop(0, 8, split_image)

        def reorder(i):
            wanted = lax.broadcasted_iota(jnp.int32, (128, 1024), 0) + i * 128
            hot = jnp.where(panels_row[...] == wanted, 1.0, 0.0).astype(BF)
            value = dot(hot, high[...])
            w1_panel[rows_at(i, 128), :] = value[:, :256] + value[:, 256:]

        loop(0, 8, reorder)

    def col_max(ref):
        return jnp.maximum(jnp.max(jnp.abs(ref[...]), axis=0, keepdims=True), 1e-30)

    def col_sums(terms):
        def add(i, carry):
            return tuple(
                c + jnp.sum(t.reshape(4, 8, 256), axis=0) for c, t in zip(carry, terms(rows_at(i, 32)))
            )

        sums = lax.fori_loop(0, 32, add, tuple(jnp.zeros((8, 256), F32) for _ in range(3)), unroll=2)
        return [jnp.sum(s, axis=0, keepdims=True) for s in sums]

    early = []

    def early_sums():
        size_p, size_a = col_max(p_slot), col_max(w1)
        inv_p, inv_a = 1.0 / size_p, 1.0 / size_a

        def terms(rows):
            p, a = p_slot[rows, :] * inv_p, w1[rows, :] * inv_a
            return p * p, p * a, a * a

        early.extend((size_p, size_a, col_sums(terms)))

    v1 = b["v0"]
    apply(0, b["v0"], w1, v1, build_rest, lambda: None)
    for swap in swaps:
        swap.wait_send()

    @pl.when(has_after)
    def _():
        basis_after.wait_send()

    @pl.when(has_before)
    def _():
        basis_before.wait_send()

    apply(1, v1, w2, None, unorder, early_sums)

    size_p, size_a, sums = early
    size_b = col_max(w2)
    inv_p, inv_a, inv_b = 1.0 / size_p, 1.0 / size_a, 1.0 / size_b

    def late_terms(rows):
        value = w2[rows, :] * inv_b
        return p_slot[rows, :] * inv_p * value, w1[rows, :] * inv_a * value, value * value

    sums = sums + col_sums(late_terms)
    sizes = [size_p, size_a, size_b]
    part, box = b["part"], b["box"]
    pairs = ((0, 0), (0, 1), (1, 1), (0, 2), (1, 2), (2, 2))
    coords = (core, x, y, z)
    axes = ("core", "x", "y", "z")

    def sum_copy(stage, k):
        i = stage * 4 + k
        here = box.at[stage, coords[stage]]
        return remote(here, here, b["sum_send"].at[i], b["sum_recv"].at[i], along(axes[stage], k))

    for stage in range(4):
        count = 2 if stage == 0 else 4
        for i in range(6):
            part[i : i + 1, :] = sums[i]
        for i in range(3):
            part[8 + i : 9 + i, :] = sizes[i]
        box[stage, coords[stage]] = part[...]
        for k in range(1, count):
            sum_copy(stage, k).start()
        for k in range(1, count):
            sum_copy(stage, k).wait_recv()
        got = [box[stage, i] for i in range(count)]
        new_sizes = []
        for i in range(3):
            top_size = got[0][8 + i : 9 + i]
            for g in got[1:]:
                top_size = jnp.maximum(top_size, g[8 + i : 9 + i])
            new_sizes.append(top_size)
        factors = [[g[8 + i : 9 + i] / new_sizes[i] for i in range(3)] for g in got]
        sums = []
        for i, (first, second) in enumerate(pairs):
            value = got[0][i : i + 1] * (factors[0][first] * factors[0][second])
            for g, f in zip(got[1:], factors[1:]):
                value = value + g[i : i + 1] * (f[first] * f[second])
            sums.append(value)
        sizes = new_sizes

    along_p, along_a, estimate = project(sums, sizes)
    est_ref[...] = estimate

    def write(i):
        rows = rows_at(i, 32)
        out_ref[rows, :] = along_p * pot_ref[rows, :] + along_a * w1_panel[rows, :]

    loop(0, 32, write, 4)
    for stage in range(4):
        for k in range(1, 2 if stage == 0 else 4):
            sum_copy(stage, k).wait_send()


def both_steps(smem_args, vmem_args, hbm_args):
    smem = pl.BlockSpec(memory_space=pltpu.SMEM)
    vmem = pl.BlockSpec(memory_space=pltpu.VMEM)
    anywhere = pl.BlockSpec(memory_space=pl.ANY)
    return pl.pallas_call(
        steps_kernel,
        out_shape=(jax.ShapeDtypeStruct((1024, 256), F32), jax.ShapeDtypeStruct((1, 256), F32)),
        in_specs=[smem] * len(smem_args) + [vmem] * len(vmem_args) + [anywhere] * len(hbm_args),
        out_specs=(vmem, vmem),
        scratch_shapes=list(BUFFERS.values()),
        compiler_params=pltpu.CompilerParams(
            collective_id=1, has_side_effects=True, vmem_limit_bytes=60 * 1024 * 1024
        ),
        name="both_steps",
    )(*smem_args, *vmem_args, *hbm_args)


def least_squares(beta_norm, first_diag, first_below, second_top, second_diag, second_below):
    first_radius = jnp.sqrt(first_diag * first_diag + first_below * first_below)
    first_cos = first_diag / first_radius
    first_sin = first_below / first_radius
    upper_term = first_cos * second_top + first_sin * second_diag
    lower_term = first_cos * second_diag - first_sin * second_top
    second_radius = jnp.sqrt(lower_term * lower_term + second_below * second_below)
    second_cos = lower_term / second_radius
    second_sin = second_below / second_radius
    weight_two = -first_sin * beta_norm * second_cos / second_radius
    weight_one = (first_cos * beta_norm - upper_term * weight_two) / first_radius
    return (weight_one, weight_two, first_sin * second_sin * beta_norm)


def project(sums, sizes):
    pp, pa, aa, pb, ab, bb = sums
    size_p, size_a, size_b = sizes
    beta = jnp.sqrt(size_p * size_p * pp + EPS)
    scale_p, scale_a, scale_b = size_p / beta, size_a / beta, size_b / beta
    first_first = scale_p * scale_p * pp
    first_image = scale_p * scale_a * pa
    first_diag = first_image
    image_image = scale_a * scale_a * aa
    rest = image_image - first_diag * first_diag * (2.0 - first_first)
    first_below = jnp.sqrt(jnp.maximum(rest, 0.0) + EPS)
    inverse = 1.0 / first_below
    first_second = (first_image - first_diag * first_first) * inverse
    second_second = jnp.maximum(rest, 0.0) * inverse * inverse
    scale_two = scale_b * inverse
    diag_two = first_diag * inverse
    first_b = scale_p * scale_two * pb
    a_b = scale_a * scale_two * ab
    b_b = scale_two * scale_two * bb
    second_top = first_b - diag_two * first_image
    image_image_two = a_b - diag_two * image_image
    second_diag = (image_image_two - first_diag * second_top) * inverse
    square = b_b - 2.0 * diag_two * a_b + diag_two * diag_two * image_image
    rest_two = (
        square
        - second_top * second_top * (2.0 - first_first)
        - second_diag * second_diag * (2.0 - second_second)
        + 2.0 * second_top * second_diag * first_second
    )
    second_below = jnp.sqrt(jnp.maximum(rest_two, 0.0) + EPS)
    weight_one, weight_two, estimate = least_squares(
        beta, first_diag, first_below, second_top, second_diag, second_below
    )
    along_a = weight_two * inverse / beta
    along_p = weight_one / beta - along_a * first_diag
    return along_p, along_a, estimate


def on_device(
    potentials,
    leaf_panels,
    near_blocks,
    near_target,
    near_source,
    near_count,
    leaf_basis,
    far_leaf,
    far_leaf_target,
    far_leaf_source,
    leaf_transfer,
    leaf_parent,
    far_two,
    far_two_target,
    far_two_source,
    two_transfer,
    two_parent,
    far_one,
    far_one_target,
    far_one_source,
):
    group = lax.axis_index("grp")
    c_mat, fl_mat = combine(
        near_target, near_source, near_count, far_leaf_target, far_leaf_source, near_blocks, far_leaf
    )
    numbers = jnp.zeros((8, 128), jnp.int32)
    numbers = numbers.at[0, :16].set(far_two_target[0]).at[1, :16].set(far_two_source[0])
    numbers = numbers.at[2, :8].set(leaf_parent)
    numbers = numbers.at[3, :32].set(lax.dynamic_slice_in_dim(two_parent, group * 32, 32, 0))
    own_two = lax.dynamic_slice_in_dim(two_transfer, group * 32, 32, 0)
    solution_part, estimate = both_steps(
        (numbers, far_one_target, far_one_source),
        (
            numbers,
            leaf_panels,
            leaf_panels.reshape(1024, 1),
            potentials,
            leaf_basis,
            leaf_transfer,
            far_two,
            own_two,
            far_one,
        ),
        (c_mat, fl_mat),
    )
    return solution_part, estimate[0]


def solution(mesh):
    both = P(("grp", "leaf"))
    in_specs = (both,) * 15 + (P(),) * 5
    return jax.shard_map(
        on_device, mesh=mesh, in_specs=in_specs, out_specs=(both, P()), check_vma=False
    )
```

time: 1200 us -> 185 us (0.15)
  blocking collectives: 690 us -> 0 us
  waiting for transfers between devices: 192 us -> 0 us
  Pallas kernels: 0 us -> 169 us
  matrix products: 140 us -> 0 us
  local copies, waits for them, and re-layouts: 116 us -> 13.6 us
  other arithmetic: 34.1 us -> 0 us
  between operations: 15.6 us -> 1.4 us
    psum x8 -> x0, blocking collectives: 690 us -> none  [the longest x2 301 us: apply(): group_total = lax.psum(partial_value, 'leaf').astype(jnp.bfloat16)]
    psum x2 -> x0, waiting for transfers between devices: 172 us -> none  [apply(): level_two = (lax.psum(far_sum, 'leaf') + falling).astype(jnp.bfloat16)]
    pallas_call x0 -> x2, Pallas kernels: none -> 169 us  [the longest x1 151 us: both_steps(): pl.pallas_call(steps_kernel, out_shape=(jax.ShapeDtypeStruct((1024, 256),...]
    dot_general x31 -> x0, matrix products: 140 us -> none  [the longest x2 31.2 us: apply(): leaf_local = jnp.einsum('tj,jar->tar', leaf_select, pieces, precision=HIGH)]
    gather x12 -> x0, local copies, waits for them, and re-layouts: 40.3 us -> none  [the longest x2 17 us: apply(): jnp.take(coeff_window, far_leaf_source[0], axis=0)]
    unnamed x112 -> x18, local copies, waits for them, and re-layouts: 30.8 us -> 11.6 us
    all_gather x2 -> x0, waiting for transfers between devices: 18.1 us -> none  [apply(): sources = lax.all_gather(group_total, 'grp', axis=0, tiled=True)]
    dot_general x1 -> x0, local copies, waits for them, and re-layouts: 15.9 us -> none  [on_device(): jnp.dot(pair_select, near_blocks.reshape(slot_total, P_SIZE * P_SIZE), pr...]
  transfers between devices with their start and end apart: 8 -> 0, of which waited for: 4 -> 0; matrix products, arithmetic and copies ran while one was open for 13% -> 0% of each run, Pallas kernels for 0% -> 0%
where the time goes in v2:
time: 185 us; the launch traced here: 184 us
  Pallas kernels  169 us (91%)
  local copies, waits for them, and re-layouts  13.6 us (7%)
    pallas_call x1, Pallas kernels, both_steps(): pl.pallas_call(steps_kernel, out_shape=(jax.ShapeDtypeStruct((1024, 256),...  151 us
    pallas_call x1, Pallas kernels, combine(): pl.pallas_call(combine_kernel, grid=(NEAR_STEPS,), out_shape=(jax.ShapeDt...  18 us
    unnamed x18, local copies, waits for them, and re-layouts  11.6 us

profile of v2, /device:TPU:0, one launch (start us, length us, event | category | flops | bytes accessed | tf_op | source)
XLA Modules:
  0.0 184.2 jit_solution(7983902345624568516)
XLA Ops:
  0.6 0.0 copy-start
  0.6 0.0 copy-start.6
  0.7 0.0 copy-start.3
  0.7 0.0 copy-start.4
  0.7 0.0 copy-start.5
  0.7 1.2 copy-done
  1.9 0.4 constant_dynamic-slice_fusion
  2.2 1.7 copy.27.two_ref
  3.9 0.0 copy-done.6
  3.9 0.1 dynamic-slice_bitcast_fusion
  4.0 0.0 copy-done.3
  4.0 0.0 copy-done.4
  4.0 0.2 scatter.15
  4.2 0.0 copy-done.5
  4.2 0.2 scatter.16
  4.4 0.2 scatter.19.numbers_s.numbers_ref
  4.6 0.0 copy-start.1
  4.6 5.2 %copy.25.far_ref = bf16[192,64,64]{2,1,0:T(8,128)(2,1)} copy(bf16[192,64,64]{0,2,1:T(8,128)(2,1)} %param.35) | data formatting | bytes 3145728 | tf_op args[7]
  10.5 0.0 copy-start.2
  10.5 18.0 %combine.1 = (bf16[1024,3072]{1,0:T(8,128)(2,1)}, bf16[512,1536]{1,0:T(8,128)(2,1)}) custom-call(s32[1,384]{1,0:T(1,128)} %near_target.1, s32[1,384]{1,0:T(1,128)} %near_source.1, s32[1]{0:T(128)S(6)} %copy.33.near_count, s32[1,192]{1,0:T(1,128)} %far_target.1, s32[1,192]{1,0:T(1,128)} %far_source.1, bf16[384,128,128]{2,1,0:T(8,128)(2,1)} %near_ref.1, ...), custom_call_target="tpu_custom_call" | custom-call | flops 10000000 | bytes 20000000 | tf_op jit(solution)/shard_map/combine/pallas_call | solution.py:83
  28.5 1.0 copy.26.panels_col
  29.6 151.2 %both_steps.1 = (f32[1024,256]{1,0:T(8,128)}, f32[1,256]{1,0:T(1,128)}) custom-call(s32[8,128]{1,0:T(8,128)} %copy-done.1, s32[32]{0:T(128)} %one_target_s.1, s32[32]{0:T(128)} %one_source_s.1, s32[8,128]{1,0:T(8,128)} %copy-done.1, s32[1,1024]{1,0:T(1,128)} %panels_row.1, s32[1024,1]{1,0:T(8,128)} %copy.26.panels_col, f32[1024,256]{1,0:T(8,128)} %pot_ref.1, ...), custom_call_target="tpu_custom_call" | custom-call | tf_op jit(solution)/shard_map/both_steps/pallas_call | solution.py:794
  180.8 2.3 %copy.34 = f32[1024,256]{1,0:T(8,128)} copy(f32[1024,256]{1,0:T(8,128)} %get-tuple-element.60) | data formatting | bytes 2097152
  183.0 1.2 copy.35
  (3 shorter events, 0.0 us)
Async XLA Ops:
  0.6 1.2 copy-start
  0.6 3.3 %copy-start.6 = (s32[128]{0:T(128)S(1)}, s32[128]{0:T(128)}, u32[]{:S(2)}) copy-start(s32[128]{0:T(128)} %param.44) | copy-start | bytes 1540
  0.7 3.3 %copy-start.3 = (s32[1,16]{1,0:T(1,128)S(1)}, s32[1,16]{1,0:T(1,128)}, u32[]{:S(2)}) copy-start(s32[1,16]{1,0:T(1,128)} %param.41) | copy-start | bytes 196
  0.7 3.3 %copy-start.4 = (s32[1,16]{1,0:T(1,128)S(1)}, s32[1,16]{1,0:T(1,128)}, u32[]{:S(2)}) copy-start(s32[1,16]{1,0:T(1,128)} %param.42) | copy-start | bytes 196
  0.7 3.5 %copy-start.5 = (s32[8]{0:T(128)S(1)}, s32[8]{0:T(128)}, u32[]{:S(2)}) copy-start(s32[8]{0:T(128)} %param.39) | copy-start | bytes 100
  4.6 23.9 %copy-start.1 = (s32[8,128]{1,0:T(8,128)}, s32[8,128]{1,0:T(8,128)S(1)}, u32[]{:S(2)}) copy-start(s32[8,128]{1,0:T(8,128)S(1)} %scatter.19.numbers_s.numbers_ref) | copy-start | bytes 12292
  10.5 18.1 %copy-start.2 = (s32[1,1024]{1,0:T(1,128)S(1)}, s32[1,1024]{1,0:T(1,128)}, u32[]{:S(2)}) copy-start(s32[1,1024]{1,0:T(1,128)} %panels_row.1) | copy-start | bytes 12292

commit v3 on v2

--- a/solution.py
+++ b/solution.py
@@ -22,7 +22,19 @@
 
 
 def combine_kernel(
-    near_target, near_source, near_count, far_target, far_source, near_ref, far_ref, c_ref, fl_ref, acc, facc
+    near_target,
+    near_source,
+    near_count,
+    far_target,
+    far_source,
+    near_ref,
+    far_ref,
+    c_hbm,
+    fl_ref,
+    acc,
+    stage,
+    far_sum,
+    sems,
 ):
     step = pl.program_id(0)
     per_step = near_ref.shape[0]
@@ -32,7 +44,6 @@
     def _():
         def zero(i, carry):
             acc[i] = jnp.zeros((P_SIZE, P_SIZE), F32)
-            facc[i] = jnp.zeros((K, K), F32)
             return carry
 
         lax.fori_loop(0, acc.shape[0], zero, 0, unroll=8)
@@ -47,39 +58,59 @@
 
     lax.fori_loop(0, live, add, 0)
 
+    keys = far_target[...] * window + far_source[...]
+    row = lax.broadcasted_iota(jnp.int32, (96, keys.shape[1]), 0)
+    wanted = (row % 8) * window + 2 * (row // 8)
+    even = jnp.where(keys == wanted, 1.0, 0.0).astype(BF)
+    odd = jnp.where(keys == wanted + 1, 1.0, 0.0).astype(BF)
+    per_far = K // NEAR_STEPS
+    turned = (((1,), (1,)), ((), ()))
+    for i in range(per_far):
+        a = step * per_far + i
+        block = far_ref[i]
+        both = jnp.concatenate(
+            [
+                lax.dot_general(even, block, turned, preferred_element_type=F32),
+                lax.dot_general(odd, block, turned, preferred_element_type=F32),
+            ],
+            axis=1,
+        )
+        for s in range(window // 2):
+            far_sum[pl.ds(s * 512 + a, 8, stride=K), :] = both[8 * s : 8 * s + 8]
+
     @pl.when(step == pl.num_programs(0) - 1)
     def _():
-        def add_far(j, carry):
-            key = far_target[0, j] * window + far_source[0, j]
-            facc[key] = facc[key] + far_ref[j].astype(F32)
+        copies = []
+        for t in range(8):
+            rows = pl.ds(t * P_SIZE, P_SIZE)
+
+            def write(s, carry, t=t, rows=rows):
+                lanes = pl.ds(pl.multiple_of(s * P_SIZE, P_SIZE), P_SIZE)
+                stage[rows, lanes] = acc[t * window + s].astype(BF)
+                return carry
+
+            lax.fori_loop(0, window, write, 0, unroll=8)
+            copies.append(pltpu.make_async_copy(stage.at[rows], c_hbm.at[rows], sems.at[t]))
+            copies[-1].start()
+
+        def write_far(i, carry):
+            rows = pl.ds(pl.multiple_of(i * 16, 16), 16)
+            for s in range(window // 2):
+                part = far_sum[pl.ds(pl.multiple_of(s * 512 + i * 16, 16), 16), :]
+                fl_ref[rows, pl.ds(s * P_SIZE, P_SIZE)] = part.astype(BF)
             return carry
 
-        lax.fori_loop(0, far_ref.shape[0], add_far, 0, unroll=4)
-
-        def write(i, carry):
-            t, s = i // window, i % window
-            rows = pl.ds(pl.multiple_of(t * P_SIZE, P_SIZE), P_SIZE)
-            lanes = pl.ds(pl.multiple_of(s * P_SIZE, P_SIZE), P_SIZE)
-            c_ref[rows, lanes] = acc[i].astype(BF)
-            return carry
-
-        lax.fori_loop(0, acc.shape[0], write, 0, unroll=8)
-
-        def write_far(i, carry):
-            t, s = i // (window // 2), i % (window // 2)
-            rows = pl.ds(pl.multiple_of(t * K, K), K)
-            lanes = pl.ds(pl.multiple_of(s * 2 * K, 2 * K), 2 * K)
-            both = jnp.concatenate([facc[2 * i], facc[2 * i + 1]], axis=1)
-            fl_ref[rows, lanes] = both.astype(BF)
-            return carry
-
-        lax.fori_loop(0, facc.shape[0] // 2, write_far, 0, unroll=8)
+        lax.fori_loop(0, 32, write_far, 0, unroll=2)
+        for copy in copies:
+            copy.wait()
 
 
 def combine(near_target, near_source, near_count, far_target, far_source, near_blocks, far_leaf):
     smem = pl.BlockSpec(memory_space=pltpu.SMEM)
+    vmem = pl.BlockSpec(memory_space=pltpu.VMEM)
     slots = near_blocks.shape[0]
     per_step = slots // NEAR_STEPS
+    far_turned = jnp.transpose(far_leaf, (1, 2, 0))
     return pl.pallas_call(
         combine_kernel,
         grid=(NEAR_STEPS,),
@@ -87,22 +118,28 @@
             jax.ShapeDtypeStruct((1024, 3072), BF),
             jax.ShapeDtypeStruct((512, 1536), BF),
         ),
-        in_specs=[smem] * 5
+        in_specs=[smem] * 3
+        + [vmem] * 2
         + [
             pl.BlockSpec((per_step, P_SIZE, P_SIZE), lambda i: (i, 0, 0)),
-            pl.BlockSpec(far_leaf.shape, lambda i: (0, 0, 0)),
+            pl.BlockSpec((K // NEAR_STEPS,) + far_turned.shape[1:], lambda i: (i, 0, 0)),
         ],
         out_specs=(
-            pl.BlockSpec((1024, 3072), lambda i: (0, 0)),
+            pl.BlockSpec(memory_space=pl.ANY),
             pl.BlockSpec((512, 1536), lambda i: (0, 0)),
         ),
-        scratch_shapes=[VMEM((192, P_SIZE, P_SIZE), F32), VMEM((192, K, K), F32)],
+        scratch_shapes=[
+            VMEM((192, P_SIZE, P_SIZE), F32),
+            VMEM((1024, 3072), BF),
+            VMEM((6144, P_SIZE), F32),
+            DMA((8,)),
+        ],
         compiler_params=pltpu.CompilerParams(
             vmem_limit_bytes=56 * 1024 * 1024, dimension_semantics=("arbitrary",)
         ),
         cost_estimate=pl.CostEstimate(flops=10**7, bytes_accessed=20 * 10**6, transcendentals=0),
         name="combine",
-    )(near_target, near_source, near_count, far_target, far_source, near_blocks, far_leaf)
+    )(near_target, near_source, near_count, far_target, far_source, near_blocks, far_turned)
 
 
 def remote(src, dst, send, recv, device):
@@ -138,24 +175,30 @@
 BUFFERS = dict(
     c_mat=VMEM((1024, 3072), BF),
     fl_mat=VMEM((512, 1536), BF),
-    tv_mat=VMEM((16, 192, 1024), BF),
+    tv_mat=VMEM((16, 128, 1024), BF),
     s_mat=VMEM((16, 128, 2048), BF),
     down_mat=VMEM((1024, 2048), BF),
     top_mat=VMEM((128, 2048), BF),
+    turned=VMEM((4096, 128), F32),
+    two=VMEM((128, K, K), BF),
+    top_sums=VMEM((16, 128, K), BF),
+    top_all=VMEM((128, 8192), BF),
     up=VMEM((K, 1024), BF),
-    composite=VMEM((K, 1024), BF),
     far_flat=VMEM((K, 2048), BF),
     transfer=VMEM((16, K, K), BF),
     far_all=VMEM((32, K, K), BF),
     basis=VMEM((24, K, P_SIZE), BF),
-    other_numbers=VMEM((8, 128), jnp.int32),
-    other_s=pltpu.SMEM((8, 128), jnp.int32),
+    other_target=VMEM((1, 16), jnp.int32),
+    other_source=VMEM((1, 16), jnp.int32),
+    other_parent=VMEM((1, 8), jnp.int32),
+    target_o=pltpu.SMEM((1, 16), jnp.int32),
+    source_o=pltpu.SMEM((1, 16), jnp.int32),
+    parent_o=pltpu.SMEM((1, 8), jnp.int32),
     v0=VMEM((1024, 256), BF),
     p_slot=VMEM((1024, 256), F32),
     w1=VMEM((1024, 256), F32),
     w2=VMEM((1024, 256), F32),
     high=VMEM((1024, 512), BF),
-    w1_panel=VMEM((1024, 256), F32),
     part=VMEM((16, 256), F32),
     box=VMEM((4, 4, 16, 256), F32),
     win=VMEM((2, 3072, 256), BF),
@@ -163,10 +206,8 @@
     chalf=VMEM((2, 512, HALF), BF),
     c2=VMEM((2, 1024, HALF), BF),
     local_half=VMEM((2, 512, HALF), F32),
-    rs_out=VMEM((16, 192, HALF), BF),
-    rs_in=VMEM((2, 16, 192, HALF), BF),
-    q1x=VMEM((2, 4, K, HALF), BF),
-    q1=VMEM((2, 16, K, HALF), BF),
+    rs_out=VMEM((16, 128, HALF), BF),
+    rs_in=VMEM((2, 16, 128, HALF), BF),
     ag0=VMEM((2, 64, 48, HALF), BF),
     ag1=VMEM((2, 64, 48, HALF), BF),
     ag2=VMEM((2, 64, 32, HALF), BF),
@@ -178,25 +219,21 @@
     sib_out=VMEM((512, HALF), BF),
     sib_in=VMEM((2, 512, HALF), BF),
     merged=VMEM((2, 512, HALF), BF),
-    load_sem=DMA((3,)),
-    ex_send=DMA((5,)),
-    ex_recv=DMA((5,)),
-    win_send=DMA((2, 2)),
-    win_recv=DMA((2, 2)),
+    load_sem=DMA((5,)),
+    ex_send=DMA((7,)),
+    ex_recv=DMA((7,)),
+    win_send=DMA((2, 4)),
+    win_recv=DMA((2, 4)),
     sib_send=DMA((2, 2)),
     sib_recv=DMA((2, 2)),
-    rs_send=DMA((2, 16)),
-    rs_recv=DMA((2, 16)),
-    q1x_send=DMA((2, 4)),
-    q1x_recv=DMA((2, 4)),
-    q1_send=DMA((2, 16)),
-    q1_recv=DMA((2, 16)),
+    rs_send=DMA((2, 32)),
+    rs_recv=DMA((2, 32)),
     ag_send=DMA((2, 27)),
     ag_recv=DMA((2, 27)),
-    far_send=DMA((2, 16)),
-    far_recv=DMA((2, 16)),
-    l2_send=DMA((2, 16)),
-    l2_recv=DMA((2, 16)),
+    far_send=DMA((2, 32)),
+    far_recv=DMA((2, 32)),
+    l2_send=DMA((2, 32)),
+    l2_recv=DMA((2, 32)),
     sum_send=DMA((16,)),
     sum_recv=DMA((16,)),
 )
@@ -204,12 +241,16 @@
 
 
 def steps_kernel(
-    numbers_s,
+    target_s,
+    source_s,
+    parent_s,
+    two_parent_s,
     one_target_s,
     one_source_s,
-    numbers_ref,
+    target_ref,
+    source_ref,
+    parent_ref,
     panels_row,
-    panels_col,
     pot_ref,
     basis_ref,
     transfer_ref,
@@ -218,13 +259,13 @@
     one_ref,
     c_hbm,
     fl_hbm,
-    out_ref,
-    est_ref,
+    w1_panel,
+    weights_ref,
     *scratch,
 ):
     b = dict(zip(NAMES, scratch))
-    basis, transfer, far_all, other_s = b["basis"], b["transfer"], b["far_all"], b["other_s"]
-    up, composite, far_flat = b["up"], b["composite"], b["far_flat"]
+    basis, transfer, far_all = b["basis"], b["transfer"], b["far_all"]
+    up, far_flat = b["up"], b["far_flat"]
     tv_mat, s_mat, down_mat, top_mat = b["tv_mat"], b["s_mat"], b["down_mat"], b["top_mat"]
     x, z, y, core = place()
     chip = z * 4 + y
@@ -244,6 +285,7 @@
     has_after = me < 127
 
     def plane(k):
+        k = lax.rem(5 * k, 16)
         tz = lax.rem(z + lax.div(k, 4), 4)
         ty = lax.rem(y + lax.rem(k, 4), 4)
         return tz * 4 + ty, (x, leaf_of(tz, ty, core))
@@ -288,8 +330,10 @@
 
     def order(i):
         rows = rows_at(i, 128)
-        wanted = lax.broadcasted_iota(jnp.int32, (128, 1024), 1)
-        hot = jnp.where(panels_col[rows, :] == wanted, 1.0, 0.0).astype(BF)
+        wanted = lax.broadcasted_iota(jnp.int32, (128, 128), 1).astype(F32)
+        column = jnp.broadcast_to(panels_row[:, rows].astype(F32), (128, 128)).T
+        hot = [jnp.where(column == wanted + 128.0 * q, 1.0, 0.0).astype(BF) for q in range(8)]
+        hot = jnp.concatenate(hot, axis=1)
         value = dot(hot, high[...])
         b["v0"][rows, :] = value[:, :256].astype(BF)
         b["p_slot"][rows, :] = value[:, :256] + value[:, 256:]
@@ -321,7 +365,9 @@
 
     ex_send, ex_recv = b["ex_send"], b["ex_recv"]
     swaps = [
-        remote(numbers_ref, b["other_numbers"], ex_send.at[0], ex_recv.at[0], sibling),
+        remote(target_ref, b["other_target"], ex_send.at[0], ex_recv.at[0], sibling),
+        remote(source_ref, b["other_source"], ex_send.at[5], ex_recv.at[5], sibling),
+        remote(parent_ref, b["other_parent"], ex_send.at[6], ex_recv.at[6], sibling),
         remote(transfer_ref, transfer.at[pl.ds(8, 8)], ex_send.at[1], ex_recv.at[1], sibling),
         remote(far_ref, far_all.at[pl.ds(16, 16)], ex_send.at[2], ex_recv.at[2], sibling),
     ]
@@ -338,8 +384,15 @@
     def _():
         basis_before.start()
 
+    numbers = (
+        (target_s, b["target_o"]),
+        (source_s, b["source_o"]),
+        (parent_s, b["parent_o"]),
+    )
+
     def number(row, i, count):
-        return numbers_s[row, i] if i < count else other_s[row, i - count]
+        own, other = numbers[row]
+        return own[0, i] if i < count else other[0, i - count]
 
     def spread(values, lanes):
         index = lax.broadcasted_iota(jnp.int32, (1, lanes), 1) // K
@@ -352,33 +405,30 @@
         return jnp.where(found == value, 1.0, 0.0).astype(BF)
 
     def build_up():
-        for swap in swaps[:2]:
+        for swap in swaps[:4]:
             swap.wait_recv()
-        fetch = pltpu.make_async_copy(b["other_numbers"], other_s, b["load_sem"].at[2])
-        fetch.start()
-        fetch.wait()
+        fetches = [
+            pltpu.make_async_copy(b["other_" + name], b[name + "_o"], b["load_sem"].at[2 + i])
+            for i, name in enumerate(("target", "source", "parent"))
+        ]
+        for fetch in fetches:
+            fetch.start()
+        for fetch in fetches:
+            fetch.wait()
         parents = [number(2, l, 8) for l in range(16)]
         for i in range(8):
             lanes = pl.ds(i * 128, 128)
             pair = transfer[pl.ds(2 * i, 2)].reshape(128, K)
             up[:, lanes] = pair.astype(F32).T.astype(BF)
-            both = [dot(transfer[2 * i + h], two_ref[parents[2 * i + h]]) for h in range(2)]
-            composite[:, lanes] = jnp.concatenate(both, axis=0).T.astype(BF)
         parent_lanes = spread(parents, 1024)
-        top_lanes = spread([numbers_s[3, parent] for parent in parents], 1024)
 
         def build(c):
             tv_mat[c // 2, rows_at(c % 2, K), :] = up[...] * chosen(parent_lanes, c)
 
         loop(0, 32, build)
 
-        def build_top(u):
-            tv_mat[u, pl.ds(128, K), :] = composite[...] * chosen(top_lanes, u)
-
-        loop(0, 16, build_top)
-
     def build_rest():
-        swaps[2].wait_recv()
+        swaps[4].wait_recv()
         targets = [number(0, j, 16) for j in range(32)]
         for i in range(16):
             far_flat[:, pl.ds(i * 128, 128)] = jnp.concatenate([far_all[2 * i], far_all[2 * i + 1]], axis=1)
@@ -389,6 +439,58 @@
 
         loop(0, 32, build_far)
 
+        turned, two = b["turned"], b["two"]
+
+        def turn(a):
+            block = two_ref[a].astype(F32).T
+            turned[pl.ds(a, K, stride=K), :] = jnp.concatenate([block[:K], block[K:]], axis=1)
+
+        loop(0, K, turn, 4)
+
+        def shorten(c):
+            block = turned[rows_at(c, K), :].astype(BF)
+            two[c] = block[:, :K]
+            two[K + c] = block[:, K:]
+
+        loop(0, K, shorten, 4)
+
+    def build_top():
+        one_lanes = spread([one_target_s[j] for j in range(32)], 2048)
+        for i in range(16):
+            far_flat[:, pl.ds(i * 128, 128)] = jnp.concatenate([one_ref[2 * i], one_ref[2 * i + 1]], axis=1)
+        for h in range(2):
+            wanted = two_parent_s[x * 32 + chip * 2 + h]
+            top_mat[pl.ds(h * K, K), :] = far_flat[...] * chosen(one_lanes, wanted)
+
+        turned, two, sums, top_all = (b[n] for n in ("turned", "two", "top_sums", "top_all"))
+
+        for h in range(2):
+            value = dot(two[x * 32 + chip * 2 + h], top_mat[pl.ds(h * K, K), :])
+            for i in range(16):
+                turned[pl.ds(i * 128 + h * K, K), :] = value[:, i * 128 : (i + 1) * 128]
+        source_lanes = spread([one_source_s[j] for j in range(32)], 2048)
+
+        def pick_sources(u):
+            found = jnp.where(source_lanes == u, 1.0, 0.0)
+            value = turned[pl.ds(0, 128), :] * found[:, 0:128]
+            for i in range(1, 16):
+                value = value + turned[pl.ds(i * 128, 128), :] * found[:, i * 128 : (i + 1) * 128]
+            sums[u] = (value[:, :K] + value[:, K:]).astype(BF)
+
+        loop(0, 16, pick_sources)
+
+        def whole(i):
+            pair = [
+                lax.dot_general(
+                    sums[two_parent_s[2 * i + h]], two[2 * i + h], (((1,), (1,)), ((), ())), preferred_element_type=F32
+                )
+                for h in range(2)
+            ]
+            top_all[:, rows_at(i, 128)] = jnp.concatenate(pair, axis=1).astype(BF)
+
+        loop(0, 64, whole, 4)
+
+    def build_last():
         for l in range(16):
             pair = jnp.concatenate([transfer[l], transfer[l]], axis=1)
             half = lax.broadcasted_iota(jnp.int32, (1, 128), 1) // K
@@ -399,24 +501,44 @@
 
             loop(0, 16, build_down, 4)
 
-        one_lanes = spread([one_target_s[j] for j in range(32)], 2048)
-        for i in range(16):
-            far_flat[:, pl.ds(i * 128, 128)] = jnp.concatenate([one_ref[2 * i], one_ref[2 * i + 1]], axis=1)
-        for h in range(2):
-            wanted = numbers_s[3, chip * 2 + h]
-            top_mat[pl.ds(h * K, K), :] = far_flat[...] * chosen(one_lanes, wanted)
-
-    def apply(it, v, w, wb, beside_rs, beside_far):
+    def apply(it, v, w, wb, beside_rs, beside_ag, beside_l2):
         win, chalf, c2 = b["win"].at[it], b["chalf"], b["c2"].at[it]
         local_half, cw = b["local_half"], b["cw"]
-        rs_out, rs_in, q1x, q1 = b["rs_out"], b["rs_in"].at[it], b["q1x"].at[it], b["q1"].at[it]
+        rs_out, rs_in = b["rs_out"], b["rs_in"].at[it]
         ag = [b["ag0"].at[it], b["ag1"].at[it], b["ag2"].at[it]]
         q_two, gathered = b["q_two"], b["gathered"]
         far_out, far_in, l2 = b["far_out"], b["far_in"].at[it], b["l2"].at[it]
         sib_out, sib_in, merged = b["sib_out"], b["sib_in"].at[it], b["merged"]
 
-        to_after = remote(v, win.at[pl.ds(0, 1024)], b["win_send"].at[it, 0], b["win_recv"].at[it, 0], after)
-        to_before = remote(v, win.at[pl.ds(2048, 1024)], b["win_send"].at[it, 1], b["win_recv"].at[it, 1], before)
+        def window_copy(side, half):
+            first, device = (0, after) if side == 0 else (2048, before)
+            i = side * 2 + half
+            return remote(
+                v.at[pl.ds(half * 512, 512)],
+                win.at[pl.ds(first + half * 512, 512)],
+                b["win_send"].at[it, i],
+                b["win_recv"].at[it, i],
+                device,
+            )
+
+        def window_start(half):
+            @pl.when(has_after)
+            def _():
+                window_copy(0, half).start()
+
+            @pl.when(has_before)
+            def _():
+                window_copy(1, half).start()
+
+        def window_land(half):
+            @pl.when(has_before)
+            def _():
+                window_copy(0, half).wait_recv()
+
+            @pl.when(has_after)
+            def _():
+                window_copy(1, half).wait_recv()
+
 
         def own_coeffs(i):
             part = dot(basis[8 + i], v[rows_at(i, P_SIZE), :]).astype(BF)
@@ -429,46 +551,45 @@
         )
         coeff_swap.start()
 
-        @pl.when(has_after)
-        def _():
-            to_after.start()
-
-        @pl.when(has_before)
-        def _():
-            to_before.start()
-
+        window_start(0)
+        if it == 0:
+            window_start(1)
         c2[pl.ds(0, 512), :] = chalf[core]
         win[pl.ds(1024, 1024), :] = v[...]
         if it == 0:
             build_up()
         coeff_swap.wait_recv()
 
-        def rs_copy(k):
+        rs_rows = (pl.ds(0, 96), pl.ds(96, 32))
+
+        def rs_copy(h, k):
             there, device = plane(k)
-            return remote(rs_out.at[there], rs_in.at[k], b["rs_send"].at[it, k], b["rs_recv"].at[it, k], device)
-
-        def rs_step(k):
-            there, _ = plane(k)
-            rs_out[there] = dot(tv_mat[there], c2[...]).astype(BF)
-            rs_copy(k).start()
-
-        loop(1, 16, rs_step)
+            rows, i = rs_rows[h], h * 16 + k
+            return remote(
+                rs_out.at[there, rows], rs_in.at[k, rows], b["rs_send"].at[it, i], b["rs_recv"].at[it, i], device
+            )
+
+        for h in range(2):
+
+            def rs_step(k, h=h):
+                there, _ = plane(k)
+                rs_out[there, rs_rows[h]] = dot(tv_mat[there, rs_rows[h]], c2[...]).astype(BF)
+                rs_copy(h, k).start()
+
+            loop(1, 16, rs_step)
         rs_in[0] = dot(tv_mat[chip], c2[...]).astype(BF)
         beside_rs()
 
-        def rs_sum(k, total):
-            rs_copy(k).wait_recv()
-            return total + rs_in[k].astype(F32)
-
-        total = lax.fori_loop(1, 16, rs_sum, rs_in[0].astype(F32)).astype(BF)
+        def rs_total(h):
+            def rs_sum(k, total):
+                rs_copy(h, k).wait_recv()
+                return total + rs_in[k, rs_rows[h]].astype(F32)
+
+            return lax.fori_loop(1, 16, rs_sum, rs_in[0, rs_rows[h]].astype(F32)).astype(BF)
 
         homes = ((z * 4 + y) * 4 + x, (x * 4 + z) * 4 + y, (y * 4 + x) * 4 + z)
         orders = (("x", "y", "z"), ("y", "z", "x"), ("z", "x", "y"))
         lasts = (z, x, y)
-        ag[0][homes[0]] = total[0:48]
-        ag[1][homes[1]] = total[48:96]
-        ag[2][homes[2]] = total[96:128]
-        q1x[x] = total[128:192]
 
         def ag_copy(stream, stage, k):
             if stage == 0:
@@ -491,67 +612,54 @@
             for k in range(1, 4):
                 ag_copy(stream, stage, k).wait_recv()
 
-        def q1x_copy(k):
-            return remote(q1x.at[x], q1x.at[x], b["q1x_send"].at[it, k], b["q1x_recv"].at[it, k], along("x", k))
-
-        def q1_copy(k):
-            part = q1.at[chip]
-            return remote(part, part, b["q1_send"].at[it, k], b["q1_recv"].at[it, k], plane(k)[1])
-
-        for stream in range(3):
-            ag_start(stream, 0)
-        for k in range(1, 4):
-            q1x_copy(k).start()
+        total = rs_total(0)
+        ag[0][homes[0]] = total[0:48]
+        ag[1][homes[1]] = total[48:96]
+        ag_start(0, 0)
+        ag_start(1, 0)
+        total = rs_total(1)
+        ag[2][homes[2]] = total
+        ag_start(2, 0)
         for stream in range(3):
             ag_land(stream, 0)
             ag_start(stream, 1)
-        for k in range(1, 4):
-            q1x_copy(k).wait_recv()
-        level_one = q1x[0].astype(F32) + q1x[1].astype(F32) + q1x[2].astype(F32) + q1x[3].astype(F32)
-        q1[chip] = level_one.astype(BF)
-
-        def q1_start(k):
-            q1_copy(k).start()
-
         for stream in range(3):
             ag_land(stream, 1)
             ag_start(stream, 2)
-        loop(1, 16, q1_start)
-
-        @pl.when(has_before)
-        def _():
-            to_after.wait_recv()
-            if it == 0:
-                basis_after.wait_recv()
-
-        @pl.when(has_after)
-        def _():
-            to_before.wait_recv()
-            if it == 0:
-                basis_before.wait_recv()
-
-        def window_coeffs(i):
-            cw[rows_at(i, K), :] = dot(basis[i], win[rows_at(i, P_SIZE), :]).astype(BF)
-
-        loop(0, 24, window_coeffs, 4)
+
+        beside_ag()
+
+        window_land(0)
         if it == 0:
             for load in loads:
                 load.wait()
 
-        def leaf_far(i):
-            part = dot(b["fl_mat"][rows_at(i, 128), :], cw[...])
-            local_half[0, rows_at(i, 128), :] = part[:, :HALF]
-            local_half[1, rows_at(i, 128), :] = part[:, HALF:]
-
-        loop(0, 4, leaf_far)
-
-        def near(i):
-            w[rows_at(i, 128), :] = dot(b["c_mat"][rows_at(i, 128), :], win[...])
-
-        loop(0, 8, near)
-
+            @pl.when(has_before)
+            def _():
+                basis_after.wait_recv()
+
+            @pl.when(has_after)
+            def _():
+                basis_before.wait_recv()
+
+        def window_coeffs(i):
+            cw[rows_at(i, K), :] = dot(basis[i], win[rows_at(i, P_SIZE), :]).astype(BF)
+
+        loop(0, 4, window_coeffs, 4)
+        loop(8, 20, window_coeffs, 4)
+
+        def near_dot(i, first, size):
+            return dot(b["c_mat"][rows_at(i, 128), pl.ds(first, size)], win[pl.ds(first, size), :])
+
+        def near_most(i):
+            w[rows_at(i, 128), :] = near_dot(i, 0, 512) + near_dot(i, 1024, 1536)
+
+        loop(0, 8, near_most)
         for stream in range(3):
             ag_land(stream, 2)
+
+        if it == 1:
+            window_start(1)
 
         def join(i):
             ip, g = i // 4, i % 4
@@ -565,49 +673,56 @@
         for j in range(32):
             gathered[pl.ds(j * K, K), :] = q_two[number(1, j, 16)]
 
-        def far_copy(k):
+        def far_copy(h, k):
             there, device = plane(k)
-            return remote(far_out.at[there], far_in.at[k], b["far_send"].at[it, k], b["far_recv"].at[it, k], device)
-
-        def far_step(k):
-            there, _ = plane(k)
-            far_out[there] = dot(s_mat[there], gathered[...]).astype(BF)
-            far_copy(k).start()
-
-        loop(1, 16, far_step)
+            rows, i = pl.ds(h * K, K), h * 16 + k
+            return remote(
+                far_out.at[there, rows],
+                far_in.at[k, rows],
+                b["far_send"].at[it, i],
+                b["far_recv"].at[it, i],
+                device,
+            )
+
+        for h in range(2):
+
+            def far_step(k, h=h):
+                there, _ = plane(k)
+                far_out[there, pl.ds(h * K, K)] = dot(s_mat[there, pl.ds(h * K, K)], gathered[...]).astype(BF)
+                far_copy(h, k).start()
+
+            loop(1, 16, far_step)
         own = dot(s_mat[chip], gathered[...])
 
-        def q1_land(k):
-            q1_copy(k).wait_recv()
-
-        loop(1, 16, q1_land)
-        for j in range(32):
-            gathered[pl.ds(j * K, K), :] = q1[one_source_s[j]]
-        l_one = dot(top_mat[...], gathered[...]).astype(BF)
-        falling = [dot(two_ref[chip * 2 + h], l_one[h * K : (h + 1) * K]) for h in range(2)]
-        own = own + jnp.concatenate(falling, axis=0)
-        beside_far()
-
-        def far_sum(k, total):
-            far_copy(k).wait_recv()
-            return total + far_in[k].astype(F32)
-
-        own = lax.fori_loop(1, 16, far_sum, own)
-        l2[rows_at(chip, 128), :] = own.astype(BF)
-
-        def l2_copy(k):
-            part = l2.at[rows_at(chip, 128)]
-            return remote(part, part, b["l2_send"].at[it, k], b["l2_recv"].at[it, k], plane(k)[1])
-
-        def l2_start(k):
-            l2_copy(k).start()
-
-        loop(1, 16, l2_start)
+        def fall(i, total):
+            part = q_two[pl.ds(i * 16, 16)].reshape(1024, HALF)
+            return total + dot(b["top_all"][:, rows_at(i, 1024)], part)
+
+        own = lax.fori_loop(0, 8, fall, own)
+
+        def l2_copy(h, k):
+            part = l2.at[rows_at(chip * 2 + h, K)]
+            i = h * 16 + k
+            return remote(part, part, b["l2_send"].at[it, i], b["l2_recv"].at[it, i], plane(k)[1])
+
+        for h in range(2):
+
+            def far_sum(k, total, h=h):
+                far_copy(h, k).wait_recv()
+                return total + far_in[k, pl.ds(h * K, K)].astype(F32)
+
+            half_sum = lax.fori_loop(1, 16, far_sum, own[h * K : (h + 1) * K])
+            l2[rows_at(chip * 2 + h, K), :] = half_sum.astype(BF)
+
+            def l2_start(k, h=h):
+                l2_copy(h, k).start()
+
+            loop(1, 16, l2_start)
 
         def drain(k):
-            rs_copy(k).wait_send()
-            q1_copy(k).wait_send()
-            far_copy(k).wait_send()
+            for h in range(2):
+                rs_copy(h, k).wait_send()
+                far_copy(h, k).wait_send()
 
         loop(1, 16, drain)
         coeff_swap.wait_send()
@@ -615,19 +730,38 @@
             for stage in range(3):
                 for k in range(1, 4):
                     ag_copy(stream, stage, k).wait_send()
-        for k in range(1, 4):
-            q1x_copy(k).wait_send()
-
-        @pl.when(has_after)
-        def _():
-            to_after.wait_send()
-
-        @pl.when(has_before)
-        def _():
-            to_before.wait_send()
+
+        for half in range(2):
+
+            @pl.when(has_after)
+            def _(half=half):
+                window_copy(0, half).wait_send()
+
+            @pl.when(has_before)
+            def _(half=half):
+                window_copy(1, half).wait_send()
+
+        beside_l2()
+
+        window_land(1)
+        loop(4, 8, window_coeffs, 4)
+        loop(20, 24, window_coeffs, 4)
+
+        def leaf_far(i):
+            part = dot(b["fl_mat"][rows_at(i, 128), :], cw[...])
+            local_half[0, rows_at(i, 128), :] = part[:, :HALF]
+            local_half[1, rows_at(i, 128), :] = part[:, HALF:]
+
+        loop(0, 4, leaf_far)
+
+        def near_rest(i):
+            w[rows_at(i, 128), :] = w[rows_at(i, 128), :] + near_dot(i, 512, 512) + near_dot(i, 2560, 512)
+
+        loop(0, 8, near_rest)
 
         def l2_land(k):
-            l2_copy(k).wait_recv()
+            for h in range(2):
+                l2_copy(h, k).wait_recv()
 
         loop(1, 16, l2_land)
 
@@ -664,11 +798,12 @@
         leaf_swap.wait_send()
 
         def l2_sent(k):
-            l2_copy(k).wait_send()
+            for h in range(2):
+                l2_copy(h, k).wait_send()
 
         loop(1, 16, l2_sent)
 
-    p_slot, w1, w2, w1_panel = b["p_slot"], b["w1"], b["w2"], b["w1_panel"]
+    p_slot, w1, w2 = b["p_slot"], b["w1"], b["w2"]
 
     def unorder():
         def split_image(i):
@@ -713,7 +848,7 @@
         early.extend((size_p, size_a, col_sums(terms)))
 
     v1 = b["v0"]
-    apply(0, b["v0"], w1, v1, build_rest, lambda: None)
+    apply(0, b["v0"], w1, v1, build_rest, build_top, build_last)
     for swap in swaps:
         swap.wait_send()
 
@@ -725,7 +860,7 @@
     def _():
         basis_before.wait_send()
 
-    apply(1, v1, w2, None, unorder, early_sums)
+    apply(1, v1, w2, None, unorder, early_sums, lambda: None)
 
     size_p, size_a, sums = early
     size_b = col_max(w2)
@@ -775,13 +910,9 @@
         sizes = new_sizes
 
     along_p, along_a, estimate = project(sums, sizes)
-    est_ref[...] = estimate
-
-    def write(i):
-        rows = rows_at(i, 32)
-        out_ref[rows, :] = along_p * pot_ref[rows, :] + along_a * w1_panel[rows, :]
-
-    loop(0, 32, write, 4)
+    weights_ref[0:1, :] = along_p
+    weights_ref[1:2, :] = along_a
+    weights_ref[2:3, :] = estimate
     for stage in range(4):
         for k in range(1, 2 if stage == 0 else 4):
             sum_copy(stage, k).wait_send()
@@ -793,15 +924,29 @@
     anywhere = pl.BlockSpec(memory_space=pl.ANY)
     return pl.pallas_call(
         steps_kernel,
-        out_shape=(jax.ShapeDtypeStruct((1024, 256), F32), jax.ShapeDtypeStruct((1, 256), F32)),
+        out_shape=(jax.ShapeDtypeStruct((1024, 256), F32), jax.ShapeDtypeStruct((8, 256), F32)),
         in_specs=[smem] * len(smem_args) + [vmem] * len(vmem_args) + [anywhere] * len(hbm_args),
         out_specs=(vmem, vmem),
         scratch_shapes=list(BUFFERS.values()),
         compiler_params=pltpu.CompilerParams(
-            collective_id=1, has_side_effects=True, vmem_limit_bytes=60 * 1024 * 1024
+            collective_id=1, has_side_effects=True, vmem_limit_bytes=62 * 1024 * 1024
         ),
         name="both_steps",
     )(*smem_args, *vmem_args, *hbm_args)
+
+
+def result_kernel(weights_ref, pot_ref, image_ref, out_ref, est_ref):
+    out_ref[...] = weights_ref[0:1, :] * pot_ref[...] + weights_ref[1:2, :] * image_ref[...]
+    est_ref[...] = weights_ref[2, :]
+
+
+def result(weights, potentials, image):
+    return pl.pallas_call(
+        result_kernel,
+        out_shape=(jax.ShapeDtypeStruct((1024, 256), F32), jax.ShapeDtypeStruct((256,), F32)),
+        compiler_params=pltpu.CompilerParams(vmem_limit_bytes=16 * 1024 * 1024),
+        name="result",
+    )(weights, potentials, image)
 
 
 def least_squares(beta_norm, first_diag, first_below, second_top, second_diag, second_below):
@@ -878,31 +1023,25 @@
     far_one_target,
     far_one_source,
 ):
-    group = lax.axis_index("grp")
     c_mat, fl_mat = combine(
         near_target, near_source, near_count, far_leaf_target, far_leaf_source, near_blocks, far_leaf
     )
-    numbers = jnp.zeros((8, 128), jnp.int32)
-    numbers = numbers.at[0, :16].set(far_two_target[0]).at[1, :16].set(far_two_source[0])
-    numbers = numbers.at[2, :8].set(leaf_parent)
-    numbers = numbers.at[3, :32].set(lax.dynamic_slice_in_dim(two_parent, group * 32, 32, 0))
-    own_two = lax.dynamic_slice_in_dim(two_transfer, group * 32, 32, 0)
-    solution_part, estimate = both_steps(
-        (numbers, far_one_target, far_one_source),
-        (
-            numbers,
+    own_numbers = (far_two_target, far_two_source, leaf_parent.reshape(1, 8))
+    image, weights = both_steps(
+        own_numbers + (two_parent, far_one_target, far_one_source),
+        own_numbers
+        + (
             leaf_panels,
-            leaf_panels.reshape(1024, 1),
             potentials,
             leaf_basis,
             leaf_transfer,
             far_two,
-            own_two,
+            jnp.transpose(two_transfer, (1, 2, 0)),
             far_one,
         ),
         (c_mat, fl_mat),
     )
-    return solution_part, estimate[0]
+    return result(weights, potentials, image)
 
 
 def solution(mesh):

time: 185 us -> 168 us (0.908)
  local copies, waits for them, and re-layouts: 13.6 us -> 1.92 us
  Pallas kernels: 169 us -> 164 us
    unnamed x18 -> x6, local copies, waits for them, and re-layouts: 11.6 us -> 1.92 us
    pallas_call x1, Pallas kernels: 151 us -> 146 us  [both_steps(): pl.pallas_call(steps_kernel, out_shape=(jax.ShapeDtypeStruct((1024, 256),...]
where the time goes in v3:
time: 168 us; the launch traced here: 167 us
  Pallas kernels  164 us (98%)
  local copies, waits for them, and re-layouts  1.92 us (1%)
    pallas_call x1, Pallas kernels, both_steps(): pl.pallas_call(steps_kernel, out_shape=(jax.ShapeDtypeStruct((1024, 256),...  146 us
    pallas_call x1, Pallas kernels, combine(): pl.pallas_call(combine_kernel, grid=(NEAR_STEPS,), out_shape=(jax.ShapeDt...  16.4 us

profile of v3, /device:TPU:0, one launch (start us, length us, event | category | flops | bytes accessed | tf_op | source)
XLA Modules:
  0.0 167.2 jit_solution(14876182440128843173)
XLA Ops:
  1.3 16.4 %combine.1 = (bf16[1024,3072]{1,0:T(8,128)(2,1)}, bf16[512,1536]{1,0:T(8,128)(2,1)}) custom-call(s32[1,384]{1,0:T(1,128)} %near_target.1, s32[1,384]{1,0:T(1,128)} %near_source.1, s32[1]{0:T(128)S(6)} %copy.22.near_count, s32[1,192]{1,0:T(1,128)} %far_target.1, s32[1,192]{1,0:T(1,128)} %far_source.1, bf16[384,128,128]{2,1,0:T(8,128)(2,1)} %near_ref.1, ...), custom_call_target="tpu_custom_call" | custom-call | flops 10000000 | bytes 20000000 | tf_op jit(solution)/shard_map/combine/pallas_call | solution.py:114
  17.7 0.0 copy-start
  17.7 146.5 %both_steps.1 = (f32[1024,256]{1,0:T(8,128)}, f32[8,256]{1,0:T(8,128)}) custom-call(s32[1,16]{1,0:T(1,128)} %target_ref.1, s32[1,16]{1,0:T(1,128)} %source_ref.1, s32[1,8]{1,0:T(1,128)} %bitcast.5, s32[128]{0:T(128)} %two_parent_s.1, s32[32]{0:T(128)} %one_target_s.1, s32[32]{0:T(128)} %one_source_s.1, s32[1,16]{1,0:T(1,128)} %target_ref.1, ...), custom_call_target="tpu_custom_call" | custom-call | tf_op jit(solution)/shard_map/both_steps/pallas_call | solution.py:925
  164.2 0.0 copy-done
  164.2 0.0 copy-start.1
  164.2 1.2 copy-done.1
  165.4 0.0 copy-start.2
  165.4 0.7 copy-done.2
  166.1 1.1 result.1
Async XLA Ops:
  17.7 146.5 %copy-start = (f32[1024,256]{1,0:T(8,128)S(1)}, f32[1024,256]{1,0:T(8,128)}, u32[]{:S(2)}) copy-start(f32[1024,256]{1,0:T(8,128)} %pot_ref.3) | copy-start | bytes 3145732
  164.2 1.2 copy-start.1
  165.4 0.7 copy-start.2

commit v4 on v3

--- a/solution.py
+++ b/solution.py
@@ -27,116 +27,118 @@
     near_count,
     far_target,
     far_source,
-    near_ref,
-    far_ref,
+    near_hbm,
+    far_hbm,
     c_hbm,
-    fl_ref,
+    fl_hbm,
+    blocks,
+    far_blocks,
     acc,
     stage,
     far_sum,
+    far_stage,
+    load_sems,
     sems,
 ):
-    step = pl.program_id(0)
-    per_step = near_ref.shape[0]
     window = 24
-
-    @pl.when(step == 0)
-    def _():
-        def zero(i, carry):
-            acc[i] = jnp.zeros((P_SIZE, P_SIZE), F32)
-            return carry
-
-        lax.fori_loop(0, acc.shape[0], zero, 0, unroll=8)
-
-    live = jnp.clip(near_count[0] - step * per_step, 0, per_step)
+    per_step = blocks.shape[0] // NEAR_STEPS
+    far_load = pltpu.make_async_copy(far_hbm, far_blocks, load_sems.at[NEAR_STEPS])
+    far_load.start()
+
+    def load(step):
+        part = pl.ds(step * per_step, per_step)
+        return pltpu.make_async_copy(near_hbm.at[part], blocks.at[part], load_sems.at[step])
+
+    for step in range(NEAR_STEPS):
+        load(step).start()
+
+    def zero(i, carry):
+        acc[i] = jnp.zeros((P_SIZE, P_SIZE), F32)
+        return carry
+
+    lax.fori_loop(0, acc.shape[0], zero, 0, unroll=8)
+    live = near_count[0]
 
     def add(j, carry):
-        slot = step * per_step + j
-        key = near_target[0, slot] * window + near_source[0, slot]
-        acc[key] = acc[key] + near_ref[j].astype(F32)
+        key = near_target[0, j] * window + near_source[0, j]
+        acc[key] = acc[key] + blocks[j].astype(F32)
         return carry
-
-    lax.fori_loop(0, live, add, 0)
 
     keys = far_target[...] * window + far_source[...]
     row = lax.broadcasted_iota(jnp.int32, (96, keys.shape[1]), 0)
     wanted = (row % 8) * window + 2 * (row // 8)
     even = jnp.where(keys == wanted, 1.0, 0.0).astype(BF)
     odd = jnp.where(keys == wanted + 1, 1.0, 0.0).astype(BF)
+    turned = (((1,), (1,)), ((), ()))
     per_far = K // NEAR_STEPS
-    turned = (((1,), (1,)), ((), ()))
-    for i in range(per_far):
-        a = step * per_far + i
-        block = far_ref[i]
-        both = jnp.concatenate(
-            [
-                lax.dot_general(even, block, turned, preferred_element_type=F32),
-                lax.dot_general(odd, block, turned, preferred_element_type=F32),
-            ],
-            axis=1,
-        )
-        for s in range(window // 2):
-            far_sum[pl.ds(s * 512 + a, 8, stride=K), :] = both[8 * s : 8 * s + 8]
-
-    @pl.when(step == pl.num_programs(0) - 1)
-    def _():
-        copies = []
-        for t in range(8):
-            rows = pl.ds(t * P_SIZE, P_SIZE)
-
-            def write(s, carry, t=t, rows=rows):
-                lanes = pl.ds(pl.multiple_of(s * P_SIZE, P_SIZE), P_SIZE)
-                stage[rows, lanes] = acc[t * window + s].astype(BF)
-                return carry
-
-            lax.fori_loop(0, window, write, 0, unroll=8)
-            copies.append(pltpu.make_async_copy(stage.at[rows], c_hbm.at[rows], sems.at[t]))
-            copies[-1].start()
-
-        def write_far(i, carry):
-            rows = pl.ds(pl.multiple_of(i * 16, 16), 16)
+    far_load.wait()
+
+    def take(step, carry):
+        for i in range(per_far):
+            a = step * per_far + i
+            block = far_blocks[a]
+            both = jnp.concatenate(
+                [
+                    lax.dot_general(even, block, turned, preferred_element_type=F32),
+                    lax.dot_general(odd, block, turned, preferred_element_type=F32),
+                ],
+                axis=1,
+            )
             for s in range(window // 2):
-                part = far_sum[pl.ds(pl.multiple_of(s * 512 + i * 16, 16), 16), :]
-                fl_ref[rows, pl.ds(s * P_SIZE, P_SIZE)] = part.astype(BF)
+                far_sum[pl.ds(s * 512 + a, 8, stride=K), :] = both[8 * s : 8 * s + 8]
+        load(step).wait()
+        first = step * per_step
+        lax.fori_loop(first, jnp.clip(live, first, first + per_step), add, 0)
+        return carry
+
+    lax.fori_loop(0, NEAR_STEPS, take, 0)
+
+    def write_far(i, carry):
+        rows = pl.ds(pl.multiple_of(i * 16, 16), 16)
+        for s in range(12):
+            part = far_sum[pl.ds(pl.multiple_of(s * 512 + i * 16, 16), 16), :]
+            far_stage[rows, pl.ds(s * P_SIZE, P_SIZE)] = part.astype(BF)
+        return carry
+
+    lax.fori_loop(0, 32, write_far, 0, unroll=2)
+    copies = [pltpu.make_async_copy(far_stage, fl_hbm, sems.at[8])]
+    copies[0].start()
+    for t in range(8):
+        rows = pl.ds(t * P_SIZE, P_SIZE)
+
+        def write(s, carry, t=t, rows=rows):
+            lanes = pl.ds(pl.multiple_of(s * P_SIZE, P_SIZE), P_SIZE)
+            stage[rows, lanes] = acc[t * window + s].astype(BF)
             return carry
 
-        lax.fori_loop(0, 32, write_far, 0, unroll=2)
-        for copy in copies:
-            copy.wait()
+        lax.fori_loop(0, window, write, 0, unroll=8)
+        copies.append(pltpu.make_async_copy(stage.at[rows], c_hbm.at[rows], sems.at[t]))
+        copies[-1].start()
+    for copy in copies:
+        copy.wait()
 
 
 def combine(near_target, near_source, near_count, far_target, far_source, near_blocks, far_leaf):
     smem = pl.BlockSpec(memory_space=pltpu.SMEM)
     vmem = pl.BlockSpec(memory_space=pltpu.VMEM)
-    slots = near_blocks.shape[0]
-    per_step = slots // NEAR_STEPS
+    anywhere = pl.BlockSpec(memory_space=pl.ANY)
     far_turned = jnp.transpose(far_leaf, (1, 2, 0))
     return pl.pallas_call(
         combine_kernel,
-        grid=(NEAR_STEPS,),
-        out_shape=(
-            jax.ShapeDtypeStruct((1024, 3072), BF),
-            jax.ShapeDtypeStruct((512, 1536), BF),
-        ),
-        in_specs=[smem] * 3
-        + [vmem] * 2
-        + [
-            pl.BlockSpec((per_step, P_SIZE, P_SIZE), lambda i: (i, 0, 0)),
-            pl.BlockSpec((K // NEAR_STEPS,) + far_turned.shape[1:], lambda i: (i, 0, 0)),
-        ],
-        out_specs=(
-            pl.BlockSpec(memory_space=pl.ANY),
-            pl.BlockSpec((512, 1536), lambda i: (0, 0)),
-        ),
+        out_shape=(jax.ShapeDtypeStruct((1024, 3072), BF), jax.ShapeDtypeStruct((512, 1536), BF)),
+        in_specs=[smem] * 3 + [vmem] * 2 + [anywhere] * 2,
+        out_specs=(anywhere, anywhere),
         scratch_shapes=[
+            VMEM(near_blocks.shape, BF),
+            VMEM(far_turned.shape, BF),
             VMEM((192, P_SIZE, P_SIZE), F32),
             VMEM((1024, 3072), BF),
             VMEM((6144, P_SIZE), F32),
-            DMA((8,)),
+            VMEM((512, 1536), BF),
+            DMA((NEAR_STEPS + 1,)),
+            DMA((9,)),
         ],
-        compiler_params=pltpu.CompilerParams(
-            vmem_limit_bytes=56 * 1024 * 1024, dimension_semantics=("arbitrary",)
-        ),
+        compiler_params=pltpu.CompilerParams(vmem_limit_bytes=60 * 1024 * 1024),
         cost_estimate=pl.CostEstimate(flops=10**7, bytes_accessed=20 * 10**6, transcendentals=0),
         name="combine",
     )(near_target, near_source, near_count, far_target, far_source, near_blocks, far_turned)
@@ -944,7 +946,7 @@
     return pl.pallas_call(
         result_kernel,
         out_shape=(jax.ShapeDtypeStruct((1024, 256), F32), jax.ShapeDtypeStruct((256,), F32)),
-        compiler_params=pltpu.CompilerParams(vmem_limit_bytes=16 * 1024 * 1024),
+        compiler_params=pltpu.CompilerParams(vmem_limit_bytes=60 * 1024 * 1024),
         name="result",
     )(weights, potentials, image)
 

time: 168 us -> 165 us (0.982)
  local copies, waits for them, and re-layouts: 1.92 us -> 0 us
    pallas_call x1, Pallas kernels: 16.4 us -> 13.2 us  [combine(): pl.pallas_call(combine_kernel, out_shape=(jax.ShapeDtypeStruct((1024, 307...]
    unnamed x6 -> x0, local copies, waits for them, and re-layouts: 1.92 us -> none
where the time goes in v4:
time: 165 us
  Pallas kernels  164 us (99%)
    pallas_call x1, Pallas kernels, both_steps(): pl.pallas_call(steps_kernel, out_shape=(jax.ShapeDtypeStruct((1024, 256),...  148 us
    pallas_call x1, Pallas kernels, combine(): pl.pallas_call(combine_kernel, out_shape=(jax.ShapeDtypeStruct((1024, 307...  13.2 us

profile of v4, /device:TPU:0, one launch (start us, length us, event | category | flops | bytes accessed | tf_op | source)
XLA Modules:
  0.0 165.2 jit_solution(16903005274171641984)
XLA Ops:
  1.3 13.2 %combine.1 = (bf16[1024,3072]{1,0:T(8,128)(2,1)}, bf16[512,1536]{1,0:T(8,128)(2,1)}) custom-call(s32[1,384]{1,0:T(1,128)} %near_target.1, s32[1,384]{1,0:T(1,128)} %near_source.1, s32[1]{0:T(128)S(6)} %copy.22.near_count, s32[1,192]{1,0:T(1,128)} %far_target.1, s32[1,192]{1,0:T(1,128)} %far_source.1, bf16[384,128,128]{2,1,0:T(8,128)(2,1)} %near_hbm.1, ...), custom_call_target="tpu_custom_call" | custom-call | flops 10000000 | bytes 20000000 | tf_op jit(solution)/shard_map/combine/pallas_call | solution.py:126
  14.5 148.1 %both_steps.1 = (f32[1024,256]{1,0:T(8,128)}, f32[8,256]{1,0:T(8,128)}) custom-call(s32[1,16]{1,0:T(1,128)} %target_ref.1, s32[1,16]{1,0:T(1,128)} %source_ref.1, s32[1,8]{1,0:T(1,128)} %bitcast.5, s32[128]{0:T(128)} %two_parent_s.1, s32[32]{0:T(128)} %one_target_s.1, s32[32]{0:T(128)} %one_source_s.1, s32[1,16]{1,0:T(1,128)} %target_ref.1, ...), custom_call_target="tpu_custom_call" | custom-call | tf_op jit(solution)/shard_map/both_steps/pallas_call | solution.py:927
  162.5 2.6 %result.1 = (f32[1024,256]{1,0:T(8,128)}, f32[256]{0:T(256)}) custom-call(f32[8,256]{1,0:T(8,128)} %get-tuple-element.8.weights_ref, f32[1024,256]{1,0:T(8,128)} %pot_ref.3, f32[1024,256]{1,0:T(8,128)} %get-tuple-element.9.image_ref), custom_call_target="tpu_custom_call" | custom-call | tf_op jit(solution)/shard_map/result/pallas_call | solution.py:946

commit v5 on v4

--- a/solution.py
+++ b/solution.py
@@ -21,36 +21,14 @@
     return jnp.dot(a, b, preferred_element_type=F32)
 
 
-def combine_kernel(
-    near_target,
-    near_source,
-    near_count,
-    far_target,
-    far_source,
-    near_hbm,
-    far_hbm,
-    c_hbm,
-    fl_hbm,
-    blocks,
-    far_blocks,
-    acc,
-    stage,
-    far_sum,
-    far_stage,
-    load_sems,
-    sems,
-):
+def combine_kernel(near_target, near_source, near_count, near_hbm, c_hbm, blocks, acc, stage, load_sems, sems):
     window = 24
     per_step = blocks.shape[0] // NEAR_STEPS
-    far_load = pltpu.make_async_copy(far_hbm, far_blocks, load_sems.at[NEAR_STEPS])
-    far_load.start()
-
-    def load(step):
+    loads = []
+    for step in range(NEAR_STEPS):
         part = pl.ds(step * per_step, per_step)
-        return pltpu.make_async_copy(near_hbm.at[part], blocks.at[part], load_sems.at[step])
-
-    for step in range(NEAR_STEPS):
-        load(step).start()
+        loads.append(pltpu.make_async_copy(near_hbm.at[part], blocks.at[part], load_sems.at[step]))
+        loads[-1].start()
 
     def zero(i, carry):
         acc[i] = jnp.zeros((P_SIZE, P_SIZE), F32)
@@ -64,45 +42,11 @@
         acc[key] = acc[key] + blocks[j].astype(F32)
         return carry
 
-    keys = far_target[...] * window + far_source[...]
-    row = lax.broadcasted_iota(jnp.int32, (96, keys.shape[1]), 0)
-    wanted = (row % 8) * window + 2 * (row // 8)
-    even = jnp.where(keys == wanted, 1.0, 0.0).astype(BF)
-    odd = jnp.where(keys == wanted + 1, 1.0, 0.0).astype(BF)
-    turned = (((1,), (1,)), ((), ()))
-    per_far = K // NEAR_STEPS
-    far_load.wait()
-
-    def take(step, carry):
-        for i in range(per_far):
-            a = step * per_far + i
-            block = far_blocks[a]
-            both = jnp.concatenate(
-                [
-                    lax.dot_general(even, block, turned, preferred_element_type=F32),
-                    lax.dot_general(odd, block, turned, preferred_element_type=F32),
-                ],
-                axis=1,
-            )
-            for s in range(window // 2):
-                far_sum[pl.ds(s * 512 + a, 8, stride=K), :] = both[8 * s : 8 * s + 8]
-        load(step).wait()
+    for step in range(NEAR_STEPS):
+        loads[step].wait()
         first = step * per_step
         lax.fori_loop(first, jnp.clip(live, first, first + per_step), add, 0)
-        return carry
-
-    lax.fori_loop(0, NEAR_STEPS, take, 0)
-
-    def write_far(i, carry):
-        rows = pl.ds(pl.multiple_of(i * 16, 16), 16)
-        for s in range(12):
-            part = far_sum[pl.ds(pl.multiple_of(s * 512 + i * 16, 16), 16), :]
-            far_stage[rows, pl.ds(s * P_SIZE, P_SIZE)] = part.astype(BF)
-        return carry
-
-    lax.fori_loop(0, 32, write_far, 0, unroll=2)
-    copies = [pltpu.make_async_copy(far_stage, fl_hbm, sems.at[8])]
-    copies[0].start()
+    copies = []
     for t in range(8):
         rows = pl.ds(t * P_SIZE, P_SIZE)
 
@@ -118,30 +62,25 @@
         copy.wait()
 
 
-def combine(near_target, near_source, near_count, far_target, far_source, near_blocks, far_leaf):
+def combine(near_target, near_source, near_count, near_blocks):
     smem = pl.BlockSpec(memory_space=pltpu.SMEM)
-    vmem = pl.BlockSpec(memory_space=pltpu.VMEM)
     anywhere = pl.BlockSpec(memory_space=pl.ANY)
-    far_turned = jnp.transpose(far_leaf, (1, 2, 0))
     return pl.pallas_call(
         combine_kernel,
-        out_shape=(jax.ShapeDtypeStruct((1024, 3072), BF), jax.ShapeDtypeStruct((512, 1536), BF)),
-        in_specs=[smem] * 3 + [vmem] * 2 + [anywhere] * 2,
-        out_specs=(anywhere, anywhere),
+        out_shape=jax.ShapeDtypeStruct((1024, 3072), BF),
+        in_specs=[smem] * 3 + [anywhere],
+        out_specs=anywhere,
         scratch_shapes=[
             VMEM(near_blocks.shape, BF),
-            VMEM(far_turned.shape, BF),
             VMEM((192, P_SIZE, P_SIZE), F32),
             VMEM((1024, 3072), BF),
-            VMEM((6144, P_SIZE), F32),
-            VMEM((512, 1536), BF),
-            DMA((NEAR_STEPS + 1,)),
-            DMA((9,)),
+            DMA((NEAR_STEPS,)),
+            DMA((8,)),
         ],
-        compiler_params=pltpu.CompilerParams(vmem_limit_bytes=60 * 1024 * 1024),
+        compiler_params=pltpu.CompilerParams(vmem_limit_bytes=56 * 1024 * 1024),
         cost_estimate=pl.CostEstimate(flops=10**7, bytes_accessed=20 * 10**6, transcendentals=0),
         name="combine",
-    )(near_target, near_source, near_count, far_target, far_source, near_blocks, far_turned)
+    )(near_target, near_source, near_count, near_blocks)
 
 
 def remote(src, dst, send, recv, device):
@@ -181,9 +120,11 @@
     s_mat=VMEM((16, 128, 2048), BF),
     down_mat=VMEM((1024, 2048), BF),
     top_mat=VMEM((128, 2048), BF),
-    turned=VMEM((4096, 128), F32),
+    turned=VMEM((6144, 128), F32),
     two=VMEM((128, K, K), BF),
     top_sums=VMEM((16, 128, K), BF),
+    far_chunk=VMEM((2, 16, K, 192), BF),
+    chunk_sem=DMA((2,)),
     top_all=VMEM((128, 8192), BF),
     up=VMEM((K, 1024), BF),
     far_flat=VMEM((K, 2048), BF),
@@ -259,8 +200,10 @@
     far_ref,
     two_ref,
     one_ref,
+    far_target_ref,
+    far_source_ref,
     c_hbm,
-    fl_hbm,
+    far_leaf_hbm,
     w1_panel,
     weights_ref,
     *scratch,
@@ -275,10 +218,17 @@
 
     loads = [
         pltpu.make_async_copy(c_hbm, b["c_mat"], b["load_sem"].at[0]),
-        pltpu.make_async_copy(fl_hbm, b["fl_mat"], b["load_sem"].at[1]),
     ]
     for load in loads:
         load.start()
+
+    def far_fetch(q):
+        return pltpu.make_async_copy(
+            far_leaf_hbm.at[pl.ds(q * 16, 16)], b["far_chunk"].at[q % 2], b["chunk_sem"].at[q % 2]
+        )
+
+    for q in range(2):
+        far_fetch(q).start()
 
     sibling = (x, chip * 2 + 1 - core)
     before = (lax.rem(lax.div(me + 127, 32), 4), lax.rem(me + 31, 32))
@@ -492,6 +442,31 @@
 
         loop(0, 64, whole, 4)
 
+    def add_far(quarters):
+        keys = far_target_ref[...] * 24 + far_source_ref[...]
+        row = lax.broadcasted_iota(jnp.int32, (96, 192), 0)
+        wanted = lax.rem(row, 8) * 24 + 2 * lax.div(row, 8)
+        even = jnp.where(keys == wanted, 1.0, 0.0).astype(BF)
+        odd = jnp.where(keys == wanted + 1, 1.0, 0.0).astype(BF)
+        for q in quarters:
+            far_fetch(q).wait()
+
+            def add(step, q=q):
+                for i in range(8):
+                    block = b["far_chunk"][q % 2, step * 8 + i]
+                    both = [
+                        lax.dot_general(part, block, (((1,), (1,)), ((), ())), preferred_element_type=F32)
+                        for part in (even, odd)
+                    ]
+                    both = jnp.concatenate(both, axis=1)
+                    a = q * 16 + step * 8 + i
+                    for s in range(12):
+                        b["turned"][pl.ds(s * 512 + a, 8, stride=K), :] = both[8 * s : 8 * s + 8]
+
+            loop(0, 2, add)
+            if q < 2:
+                far_fetch(q + 2).start()
+
     def build_last():
         for l in range(16):
             pair = jnp.concatenate([transfer[l], transfer[l]], axis=1)
@@ -503,7 +478,16 @@
 
             loop(0, 16, build_down, 4)
 
-    def apply(it, v, w, wb, beside_rs, beside_ag, beside_l2):
+        add_far((2, 3))
+
+        def write_far(i):
+            for s in range(12):
+                part = b["turned"][rows_at(s * 32 + i, 16), :]
+                b["fl_mat"][rows_at(i, 16), pl.ds(s * P_SIZE, P_SIZE)] = part.astype(BF)
+
+        loop(0, 32, write_far, 2)
+
+    def apply(it, v, w, wb, beside_rs, beside_ag, beside_far, beside_l2):
         win, chalf, c2 = b["win"].at[it], b["chalf"], b["c2"].at[it]
         local_half, cw = b["local_half"], b["cw"]
         rs_out, rs_in = b["rs_out"], b["rs_in"].at[it]
@@ -701,6 +685,7 @@
             return total + dot(b["top_all"][:, rows_at(i, 1024)], part)
 
         own = lax.fori_loop(0, 8, fall, own)
+        beside_far()
 
         def l2_copy(h, k):
             part = l2.at[rows_at(chip * 2 + h, K)]
@@ -850,7 +835,7 @@
         early.extend((size_p, size_a, col_sums(terms)))
 
     v1 = b["v0"]
-    apply(0, b["v0"], w1, v1, build_rest, build_top, build_last)
+    apply(0, b["v0"], w1, v1, build_rest, build_top, lambda: add_far((0, 1)), build_last)
     for swap in swaps:
         swap.wait_send()
 
@@ -862,7 +847,7 @@
     def _():
         basis_before.wait_send()
 
-    apply(1, v1, w2, None, unorder, early_sums, lambda: None)
+    apply(1, v1, w2, None, unorder, early_sums, lambda: None, lambda: None)
 
     size_p, size_a, sums = early
     size_b = col_max(w2)
@@ -1025,9 +1010,7 @@
     far_one_target,
     far_one_source,
 ):
-    c_mat, fl_mat = combine(
-        near_target, near_source, near_count, far_leaf_target, far_leaf_source, near_blocks, far_leaf
-    )
+    c_mat = combine(near_target, near_source, near_count, near_blocks)
     own_numbers = (far_two_target, far_two_source, leaf_parent.reshape(1, 8))
     image, weights = both_steps(
         own_numbers + (two_parent, far_one_target, far_one_source),
@@ -1040,8 +1023,10 @@
             far_two,
             jnp.transpose(two_transfer, (1, 2, 0)),
             far_one,
+            far_leaf_target,
+            far_leaf_source,
         ),
-        (c_mat, fl_mat),
+        (c_mat, jnp.transpose(far_leaf, (1, 2, 0))),
     )
     return result(weights, potentials, image)
 

time: 165 us -> 159 us (0.964)
  Pallas kernels: 164 us -> 157 us
    pallas_call x1, Pallas kernels: 13.2 us -> 9.57 us  [combine(): pl.pallas_call(combine_kernel, out_shape=jax.ShapeDtypeStruct((1024, 3072...]
    pallas_call x1, Pallas kernels: 148 us -> 145 us  [both_steps(): pl.pallas_call(steps_kernel, out_shape=(jax.ShapeDtypeStruct((1024, 256),...]
where the time goes in v5:
time: 159 us; the launch traced here: 158 us
  Pallas kernels  157 us (99%)
    pallas_call x1, Pallas kernels, both_steps(): pl.pallas_call(steps_kernel, out_shape=(jax.ShapeDtypeStruct((1024, 256),...  145 us
    pallas_call x1, Pallas kernels, combine(): pl.pallas_call(combine_kernel, out_shape=jax.ShapeDtypeStruct((1024, 3072...  9.57 us

profile of v5, /device:TPU:0, one launch (start us, length us, event | category | flops | bytes accessed | tf_op | source)
XLA Modules:
  0.0 158.1 jit_solution(16946878163219980911)
XLA Ops:
  1.3 9.6 %combine.1.c_hbm = bf16[1024,3072]{1,0:T(8,128)(2,1)} custom-call(s32[1,384]{1,0:T(1,128)} %near_target.1, s32[1,384]{1,0:T(1,128)} %near_source.1, s32[1]{0:T(128)S(6)} %copy.22.near_count, bf16[384,128,128]{2,1,0:T(8,128)(2,1)} %near_hbm.1), custom_call_target="tpu_custom_call" | custom-call | flops 10000000 | bytes 20000000 | tf_op jit(solution)/shard_map/combine/pallas_call | solution.py:68
  10.8 144.6 %both_steps.1 = (f32[1024,256]{1,0:T(8,128)}, f32[8,256]{1,0:T(8,128)}) custom-call(s32[1,16]{1,0:T(1,128)} %target_ref.1, s32[1,16]{1,0:T(1,128)} %source_ref.1, s32[1,8]{1,0:T(1,128)} %bitcast.5, s32[128]{0:T(128)} %two_parent_s.1, s32[32]{0:T(128)} %one_target_s.1, s32[32]{0:T(128)} %one_source_s.1, s32[1,16]{1,0:T(1,128)} %target_ref.1, ...), custom_call_target="tpu_custom_call" | custom-call | tf_op jit(solution)/shard_map/both_steps/pallas_call | solution.py:912
  155.5 2.6 %result.1 = (f32[1024,256]{1,0:T(8,128)}, f32[256]{0:T(256)}) custom-call(f32[8,256]{1,0:T(8,128)} %get-tuple-element.4.weights_ref, f32[1024,256]{1,0:T(8,128)} %pot_ref.3, f32[1024,256]{1,0:T(8,128)} %get-tuple-element.5.image_ref), custom_call_target="tpu_custom_call" | custom-call | tf_op jit(solution)/shard_map/result/pallas_call | solution.py:931

commit v6 on v5

--- a/solution.py
+++ b/solution.py
@@ -313,6 +313,12 @@
     def _():
         basis[pl.ds(16, 8)] = jnp.zeros((8, K, P_SIZE), BF)
 
+    def first_coeffs(i):
+        part = dot(basis_ref[i], b["v0"][rows_at(i, P_SIZE), :]).astype(BF)
+        b["chalf"][0, rows_at(i, K), :] = part[:, :HALF]
+        b["chalf"][1, rows_at(i, K), :] = part[:, HALF:]
+
+    loop(0, 8, first_coeffs, 8)
     pl.semaphore_wait(barrier, 19 + has_before.astype(jnp.int32) + has_after.astype(jnp.int32))
 
     ex_send, ex_recv = b["ex_send"], b["ex_recv"]
@@ -531,7 +537,8 @@
             chalf[0, rows_at(i, K), :] = part[:, :HALF]
             chalf[1, rows_at(i, K), :] = part[:, HALF:]
 
-        loop(0, 8, own_coeffs, 8)
+        if it == 1:
+            loop(0, 8, own_coeffs, 8)
         coeff_swap = remote(
             chalf.at[1 - core], c2.at[pl.ds(512, 512)], b["sib_send"].at[it, 0], b["sib_recv"].at[it, 0], sibling
         )
@@ -654,7 +661,7 @@
             q_two[g * 32 + 2 * ip] = jnp.concatenate([first, second[0:16]], axis=0)
             q_two[g * 32 + 2 * ip + 1] = jnp.concatenate([second[16:48], third], axis=0)
 
-        loop(0, 64, join, 4)
+        loop(0, 64, join, 8)
 
         for j in range(32):
             gathered[pl.ds(j * K, K), :] = q_two[number(1, j, 16)]
@@ -755,7 +762,7 @@
         def down_sibling(i):
             sib_out[rows_at(i, 128), :] = dot(down_mat[rows_at(i + 4, 128), :], l2[...]).astype(BF)
 
-        loop(0, 4, down_sibling)
+        loop(0, 4, down_sibling, 2)
         leaf_swap = remote(sib_out, sib_in, b["sib_send"].at[it, 1], b["sib_recv"].at[it, 1], sibling)
         leaf_swap.start()
 
@@ -763,7 +770,7 @@
             rows = rows_at(i, 128)
             merged[core, rows, :] = (local_half[core, rows, :] + dot(down_mat[rows, :], l2[...])).astype(BF)
 
-        loop(0, 4, down_own)
+        loop(0, 4, down_own, 2)
         leaf_swap.wait_recv()
         merged[1 - core] = (local_half[1 - core] + sib_in[...].astype(F32)).astype(BF)
 
@@ -781,7 +788,7 @@
                 if wb is not None:
                     wb[rows, lanes] = value.astype(BF)
 
-        loop(0, 8, finish, 2)
+        loop(0, 8, finish, 4)
         leaf_swap.wait_send()
 
         def l2_sent(k):

time: 159 us -> 157 us (0.987)
  no operation moved by 1% of the time
where the time goes in v6:
time: 157 us
  Pallas kernels  156 us (99%)
    pallas_call x1, Pallas kernels, both_steps(): pl.pallas_call(steps_kernel, out_shape=(jax.ShapeDtypeStruct((1024, 256),...  145 us
    pallas_call x1, Pallas kernels, combine(): pl.pallas_call(combine_kernel, out_shape=jax.ShapeDtypeStruct((1024, 3072...  8.31 us

profile of v6, /device:TPU:0, one launch (start us, length us, event | category | flops | bytes accessed | tf_op | source)
XLA Modules:
  0.0 157.0 jit_solution(3804222177018000927)
XLA Ops:
  1.3 8.3 %combine.1.c_hbm = bf16[1024,3072]{1,0:T(8,128)(2,1)} custom-call(s32[1,384]{1,0:T(1,128)} %near_target.1, s32[1,384]{1,0:T(1,128)} %near_source.1, s32[1]{0:T(128)S(6)} %copy.22.near_count, bf16[384,128,128]{2,1,0:T(8,128)(2,1)} %near_hbm.1), custom_call_target="tpu_custom_call" | custom-call | flops 10000000 | bytes 20000000 | tf_op jit(solution)/shard_map/combine/pallas_call | solution.py:68
  9.6 144.7 %both_steps.1 = (f32[1024,256]{1,0:T(8,128)}, f32[8,256]{1,0:T(8,128)}) custom-call(s32[1,16]{1,0:T(1,128)} %target_ref.1, s32[1,16]{1,0:T(1,128)} %source_ref.1, s32[1,8]{1,0:T(1,128)} %bitcast.5, s32[128]{0:T(128)} %two_parent_s.1, s32[32]{0:T(128)} %one_target_s.1, s32[32]{0:T(128)} %one_source_s.1, s32[1,16]{1,0:T(1,128)} %target_ref.1, ...), custom_call_target="tpu_custom_call" | custom-call | tf_op jit(solution)/shard_map/both_steps/pallas_call | solution.py:919
  154.3 2.6 %result.1 = (f32[1024,256]{1,0:T(8,128)}, f32[256]{0:T(256)}) custom-call(f32[8,256]{1,0:T(8,128)} %get-tuple-element.4.weights_ref, f32[1024,256]{1,0:T(8,128)} %pot_ref.3, f32[1024,256]{1,0:T(8,128)} %get-tuple-element.5.image_ref), custom_call_target="tpu_custom_call" | custom-call | tf_op jit(solution)/shard_map/result/pallas_call | solution.py:938
